TPU v7x, 32 devices: a whole 2x2x4 slice. The times are simulated.
32 devices in a mesh: clip: 2 (over y), tm: 4 (over z), head: 2 (over x), sub: 2 (over core).
Axes of the slice: x: 2, y: 2, z: 4, core: 2. Of those that a mesh axis runs over, the one named last changes fastest.
Arguments:
- queries: bfloat16 [8, 256, 3072], P(('clip', 'tm'), None, ('head', 'sub')), parts along dimension 0, may hold values from -6 to 6, as said below
- keys: bfloat16 [8, 256, 3072], P(('clip', 'tm'), None, ('head', 'sub')), parts along dimension 0, may hold values from -6 to 6, as said below
- values: bfloat16 [8, 256, 3072], P(('clip', 'tm'), None, ('head', 'sub')), parts along dimension 0, may hold values from -6 to 6
- band_table: int32 [4, 4], replicated, may hold values from 0 to 3, as said below
- windows: int32 [7], replicated, may hold values from 1 to 128, as said below
- out_weight: bfloat16 [3072, 3072], P(('head', 'sub')), may hold values from -0.109375 to 0.109375
Outputs:
- mixed: bfloat16 [8, 256, 3072], P(('clip', 'tm'), ('head', 'sub')), parts along dimension 0
There are 2 independent parts, one for each index of `clip`. A program takes and returns all parts, laid end to end along the dimension named above; an argument that names none is the same for every part. Nothing has to cross between parts.
Inputs may be any that keep to these rules, and one draw needn't show every extreme that they name: `queries`: entries of normal law within the range; some rows may be aligned with some key rows. `keys`: entries of normal law within the range; some rows may be aligned with some query rows. `band_table`: Symmetric; 0 exactly on the diagonal; off the diagonal, for frames at distance d it is floor(log2 d) + 1 or one more, never above 6; the pair of frames 0 and 3 takes the one more (up to 6). windows[0] = 128; for k >= 1, windows[k] lies between max(1, 64 // 2**k) and max(that + 1, 128 // 2**k + 1) - 1.
All inputs are finite; a program needn't handle non-finite values.
Results may differ from a plain program's by a relative error of at most 0.015.
Values may be sent and summed in bfloat16 or wider, within the bound.
No kernel may reach another device: no remote copies, remote signals or barrier semaphores. Data moves between devices by JAX's collectives and lax.ppermute only.
A program may use at most 64 MiB of HBM per device.

v0:
```python
import functools

import jax
import jax.numpy as jnp
from jax import lax
from jax.experimental import pallas as pl
from jax.experimental.pallas import tpu as pltpu
from jax.sharding import PartitionSpec as P

HEAD = 128
ANY = pl.BlockSpec(memory_space=pl.ANY)
VMEM = pl.BlockSpec(memory_space=pltpu.VMEM)
HBM = pl.BlockSpec(memory_space=pltpu.HBM)
SMEM = pl.BlockSpec(memory_space=pltpu.SMEM)
CHUNKS = 2
ACROSS = 64
PACK_MB = 59
TIE = 0
FIRST = [2]
W_AFTER = 2


def gathered(queries, keys, values, band_table, windows, out_weight):
    frames, length, width = queries.shape
    heads = width // HEAD
    scale = HEAD ** (-0.5)
    here = lax.axis_index("tm") * frames
    query = queries[0].reshape(length, heads, HEAD)
    places = lax.iota(jnp.int32, length)
    gap = jnp.abs(places[:, None] - places[None, :])

    def absorb(carry, key_frame, value_frame, frame):
        peak, total, numer = carry
        reach = windows[band_table[here, frame]]
        allowed = (gap <= reach)[None]
        scores = (
            jnp.einsum(
                "phd,qhd->hpq",
                query,
                key_frame.reshape(length, heads, HEAD),
                preferred_element_type=jnp.float32,
            )
            * scale
        )
        masked = jnp.where(allowed, scores, jnp.float32(-1e30))
        top = jnp.maximum(peak, jnp.max(masked, axis=-1))
        weights = jnp.where(allowed, jnp.exp(scores - top[:, :, None]), jnp.float32(0.0))
        shrink = jnp.exp(peak - top)
        total = total * shrink + jnp.sum(weights, axis=-1)
        added = jnp.einsum(
            "hpq,qhd->phd",
            weights.astype(jnp.bfloat16),
            value_frame.reshape(length, heads, HEAD),
            preferred_element_type=jnp.float32,
        )
        numer = numer * jnp.transpose(shrink)[:, :, None] + added
        return (top, total, numer)

    carry = (
        jnp.full((heads, length), -1e30, jnp.float32),
        jnp.zeros((heads, length), jnp.float32),
        jnp.zeros((length, heads, HEAD), jnp.float32),
    )
    key_part = lax.all_gather(keys, "tm", axis=0, tiled=True)
    value_part = lax.all_gather(values, "tm", axis=0, tiled=True)

    def advance(inner, item):
        return (absorb(inner, *item), None)

    state, _ = lax.scan(
        advance, carry, (key_part, value_part, lax.iota(jnp.int32, key_part.shape[0]))
    )
    _, total, numer = state
    attended = (
        (numer / jnp.transpose(total)[:, :, None]).astype(jnp.bfloat16).reshape(length, width)
    )
    mixed = lax.psum_scatter(
        jnp.dot(attended, out_weight, preferred_element_type=jnp.float32).astype(jnp.bfloat16),
        ("head", "sub"),
        scatter_dimension=0,
        tiled=True,
    )
    return mixed[None]


def run_copies(copies, sem):
    started = [pltpu.make_async_copy(s, d, sem.at[i]) for i, (s, d) in enumerate(copies)]
    for copy in started:
        copy.start()
    for copy in started:
        copy.wait()


def pack_kernel(n, cores, tokens, rounds, q_ref, k_ref, v_ref, *rest):
    outs, sem = rest[: len(rounds)], rest[len(rounds)]
    z = lax.axis_index("tm")
    _, half, wide = outs[0].shape
    copies = []
    for r, out in zip(rounds, outs):
        t = z ^ r
        cols = pl.ds(pl.multiple_of((t // cores) * wide, wide), wide)
        b = t % cores
        rows = pl.ds(pl.multiple_of(b * half, half), half)
        copies.append((k_ref.at[0, rows, cols], out.at[0]))
        copies.append((v_ref.at[0, rows, cols], out.at[1]))
        for i in range(half // tokens):
            place = pl.ds(pl.multiple_of(((i ^ b) * cores + b) * tokens, tokens), tokens)
            copies.append((q_ref.at[0, place, cols], out.at[2, pl.ds(i * tokens, tokens)]))
    run_copies(copies, sem)


def bias_kernel(n, cores, tokens, band_ref, reach_ref, bias_ref):
    z, c = lax.axis_index("tm"), lax.axis_index("sub")
    length = bias_ref.shape[1] // n
    half = length // cores
    t = (z % (n // cores)) * cores + c
    row = lax.broadcasted_iota(jnp.int32, (half, length), 0)
    key = lax.broadcasted_iota(jnp.int32, (half, length), 1)
    place = ((row // tokens ^ c) * cores + c) * tokens + row % tokens
    key_place = jnp.where(key < half, key + c * half, key - half + (1 - c) * half)
    gap = jnp.abs(place - key_place)
    for r in range(n):
        for s in range(n):
            reach = reach_ref[band_ref[t ^ r, t ^ s]]
            bias_ref[r * half : (r + 1) * half, s * length : (s + 1) * length] = jnp.where(
                gap <= reach, jnp.float32(0.0), jnp.float32(-1e30)
            )


RATE = HEAD ** (-0.5) * 1.4426950408889634
LAST = 1


def hidden(tokens, half, r, at, s, g):
    return tokens >= ACROSS and at == 0 and r != s and g >= half


def attend_early_kernel(n, cores, tokens, bias_ref, *rest):
    own, other = rest[:n], rest[n : 2 * n - 1]
    numer_ref, total_ref, top_ref, s_all, p_all = rest[2 * n - 1 :]
    half = own[0].shape[1]
    heads = own[0].shape[2] // HEAD
    length = half * cores
    rate = jnp.float32(RATE)
    keyed = [
        (s, g) for s in range(n) for g in range(0, length, 128) if s != LAST or g < half
    ]
    places = [(r, at) for r in range(n) for at in range(0, half, tokens)]

    def both(i, s, cols):
        mine = own[s][i, :, cols]
        if s == LAST:
            return mine
        return jnp.concatenate([mine, other[(s ^ 1) - 1][i, :, cols]])

    for slot in range(2):
        for r, at in places:
            for s, g in keyed:
                if hidden(tokens, half, r, at, s, g):
                    lines = slice(r * half + at, r * half + at + tokens)
                    p_all[slot, lines, s * length + g : s * length + g + 128] = jnp.zeros(
                        (tokens, 128), jnp.bfloat16
                    )

    def score(h, s):
        cols = slice(h * HEAD, (h + 1) * HEAD)
        q = jnp.concatenate([own[r][2, :, cols] for r in range(n)])
        k = both(0, s, cols)
        s_all[h % 2, :, s * length : s * length + k.shape[0]] = lax.dot_general(
            q, k, (((1,), (1,)), ((), ())), preferred_element_type=jnp.float32
        )

    def soften(h, r, at):
        used = [s * length + g for s, g in keyed if not hidden(tokens, half, r, at, s, g)]
        for step in range(r * half + at, r * half + at + tokens, 16):
            lines = slice(step, step + 16)
            parts = [
                s_all[h % 2, lines, g : g + 128] + bias_ref[lines, g : g + 128] for g in used
            ]
            top = jnp.max(functools.reduce(jnp.maximum, parts), axis=1, keepdims=True)
            top_ref[h, lines, :] = jnp.broadcast_to(top, (16, HEAD))
            for g, part in zip(used, parts):
                p_all[h % 2, lines, g : g + 128] = jnp.exp2((part - top) * rate).astype(
                    jnp.bfloat16
                )

    def mix(h, r):
        cols = slice(h * HEAD, (h + 1) * HEAD)
        numer = 0.0
        lines = slice(r * half, (r + 1) * half)
        for s in range(n):
            v = both(1, s, cols)
            numer += jnp.dot(
                p_all[h % 2, lines, s * length : s * length + v.shape[0]],
                jnp.concatenate([v, jnp.ones_like(v)], axis=1),
                preferred_element_type=jnp.float32,
            )
        numer_ref[h, lines, :] = numer[:, :HEAD]
        total_ref[h, lines, :] = numer[:, HEAD:]

    for s in range(n):
        score(0, s)
    for h in range(heads):
        for r in range(n):
            if h + 1 < heads:
                score(h + 1, r)
            for at in range(0, half, tokens):
                soften(h, r, at)
            mix(h, r)


def attend_late_kernel(n, cores, tokens, start, count, bias_ref, numer_ref, total_ref, top_ref, *rest):
    own, other, outs = rest[:n], rest[n], rest[n + 1 : -4]
    s_all, p_all, f_all, o_all = rest[-4:]
    z, c = lax.axis_index("tm"), lax.axis_index("sub")
    half = own[0].shape[1]
    heads = own[0].shape[2] // HEAD
    length = half * cores
    t = (z % (n // cores)) * cores + c
    rate = jnp.float32(RATE)
    first = LAST * length + half
    seen = [
        (r, at)
        for r in range(n)
        for at in range(0, half, tokens)
        if not hidden(tokens, half, r, at, LAST, half)
    ]

    def score(h):
        cols = slice(h * HEAD, (h + 1) * HEAD)
        q = jnp.concatenate([own[r][2, at + start : at + start + count, cols] for r, at in seen])
        s_all[h] = lax.dot_general(
            q, other[0, :, cols], (((1,), (1,)), ((), ())), preferred_element_type=jnp.float32
        )

    for h in range(heads):
        score(h)
    for h in range(heads):
        cols = slice(h * HEAD, (h + 1) * HEAD)
        for i, (r, at) in enumerate(seen):
            for step in range(0, count, 16):
                lines = slice(i * count + step, i * count + step + 16)
                base = r * half + at + start + step
                place = slice(base, base + 16)
                parts = [
                    s_all[h, lines, g : g + 128] + bias_ref[place, first + g : first + g + 128]
                    for g in range(0, half, 128)
                ]
                old = top_ref[h, place, :]
                top = jnp.max(functools.reduce(jnp.maximum, parts), axis=1, keepdims=True)
                top = jnp.maximum(old, top)
                f_all[h, lines, :] = jnp.exp2((old - top) * rate)
                for g, part in zip(range(0, half, 128), parts):
                    p_all[h, lines, g : g + 128] = jnp.exp2((part - top[:, :1]) * rate).astype(
                        jnp.bfloat16
                    )
        v = other[1, :, cols]
        added = jnp.dot(
            p_all[h], jnp.concatenate([v, jnp.ones_like(v)], axis=1),
            preferred_element_type=jnp.float32,
        )
        for r in range(n):
            for b, at in enumerate(range(0, half, tokens)):
                place = slice(r * half + at + start, r * half + at + start + count)
                numer, total = numer_ref[h, place, :], total_ref[h, place, :]
                if (r, at) in seen:
                    i = seen.index((r, at)) * count
                    shrink = f_all[h, i : i + count, :]
                    numer = numer * shrink + added[i : i + count, :HEAD]
                    total = total * shrink + added[i : i + count, HEAD:]
                o_all[r, b * count : (b + 1) * count, cols] = (numer / total).astype(jnp.bfloat16)

    for i, out in enumerate(outs):
        out[...] = o_all[t ^ z ^ (n - 1 - i)]


def project_kernel(n, cores, places, own_w, other_w, *rest):
    parts = rest[:n]
    keep_ref, send_ref, a_all = rest[n:]
    z, c, x = lax.axis_index("tm"), lax.axis_index("sub"), lax.axis_index("head")
    count = keep_ref.shape[0]
    for (k, first), part in zip(places, parts):
        for b in range(2):
            at = pl.ds(pl.multiple_of((b ^ 1 ^ x ^ c) * count + first, count), count)
            a_all[z ^ k, b * count : (b + 1) * count] = part[at, :]
    per = n // cores
    wide = a_all.shape[2]
    total = 0.0
    for w_ref, core in ((own_w, c), (other_w, 1 - c)):
        for g in range(per):
            total += jnp.dot(
                a_all[core * per + g], w_ref[g * wide : (g + 1) * wide, :],
                preferred_element_type=jnp.float32,
            )
    send_ref[...] = total[:count].astype(send_ref.dtype)
    keep_ref[...] = total[count:]


def add_kernel(chunks, *refs):
    out_ref = refs[-1]
    for a in range(chunks):
        keep, got = refs[2 * a], refs[2 * a + 1]
        count = keep.shape[0]
        out_ref[0, a * count : (a + 1) * count] = (
            keep[...] + got[...].astype(jnp.float32)
        ).astype(out_ref.dtype)


def swapped(x, axis):
    return lax.ppermute(x, axis, [(0, 1), (1, 0)])


def spread(n, cores, queries, keys, values, band_table, windows, out_weight):
    _, length, width = queries.shape
    depth, model = out_weight.shape
    wide = width * cores // n
    half = length // cores
    tokens = half // 2
    count = tokens // CHUNKS
    rows = 2 * count
    bf16 = queries.dtype

    def pack(rounds, mb, queries, keys, values):
        return pl.pallas_call(
            functools.partial(pack_kernel, n, cores, tokens, rounds),
            out_shape=[jax.ShapeDtypeStruct((3, half, wide), bf16)] * len(rounds),
            in_specs=[ANY] * 3,
            out_specs=[VMEM] * len(rounds),
            scratch_shapes=[pltpu.SemaphoreType.DMA((4 * len(rounds),))],
            compiler_params=pltpu.CompilerParams(vmem_limit_bytes=mb * 2**20),
            name="pack",
        )(queries, keys, values)

    packed = dict(zip(FIRST, pack(FIRST, PACK_MB, queries, keys, values)))
    others = [r for r in range(n) if r not in FIRST]
    arrays = lax.optimization_barrier((queries, keys, values, packed[FIRST[0]]))[:3]
    packed.update(zip(others, pack(others, 6, *arrays)))
    per = n // cores
    rounds = [
        [
            (z * cores + c, (c * per + (z ^ r) // cores) * cores + (z ^ r) % cores)
            for z in range(n)
            for c in range(cores)
        ]
        for r in range(n)
    ]
    bias = pl.pallas_call(
        functools.partial(bias_kernel, n, cores, tokens),
        out_shape=jax.ShapeDtypeStruct((n * half, n * length), jnp.float32),
        in_specs=[SMEM, SMEM],
        out_specs=VMEM,
        compiler_params=pltpu.CompilerParams(vmem_limit_bytes=4 * 2**20),
        name="bias",
    )(band_table, windows)
    blocks = [packed[r] for r in range(n)]
    blocks[TIE], _ = lax.optimization_barrier((packed[TIE], bias))
    own = [lax.ppermute(blocks[r], ("tm", "sub"), rounds[r]) for r in range(n)]
    weight, _ = lax.optimization_barrier((out_weight, packed[W_AFTER]))
    other_weight = swapped(weight, "sub")
    other = []
    for r in range(n):
        other.append(swapped(own[r], "sub"))
    bias, other_weight = lax.optimization_barrier((bias, other_weight))

    heads = wide // HEAD
    f32 = jnp.float32
    partial = pl.pallas_call(
        functools.partial(attend_early_kernel, n, cores, tokens),
        out_shape=[jax.ShapeDtypeStruct((heads, n * half, HEAD), f32)] * 3,
        in_specs=[VMEM] * (2 * n),
        out_specs=[VMEM] * 3,
        scratch_shapes=[
            pltpu.VMEM((2, n * half, n * length), f32),
            pltpu.VMEM((2, n * half, n * length), bf16),
        ],
        compiler_params=pltpu.CompilerParams(vmem_limit_bytes=24 * 2**20),
        name="attend_early",
    )(bias, *own, *other[1:])
    blocks_seen = 2 * n if tokens < ACROSS else n + 1
    back = []
    for a in range(CHUNKS):
        outs = pl.pallas_call(
            functools.partial(attend_late_kernel, n, cores, tokens, a * count, count),
            out_shape=[jax.ShapeDtypeStruct((rows, wide), bf16)] * n,
            in_specs=[VMEM] * (5 + n),
            out_specs=[VMEM] * n,
            scratch_shapes=[
                pltpu.VMEM((heads, blocks_seen * count, half), f32),
                pltpu.VMEM((heads, blocks_seen * count, half), bf16),
                pltpu.VMEM((heads, blocks_seen * count, HEAD), f32),
                pltpu.VMEM((n, rows, wide), bf16),
            ],
            compiler_params=pltpu.CompilerParams(vmem_limit_bytes=24 * 2**20),
            name="attend_late",
        )(bias, *partial, *own, other[0])
        for i, out in enumerate(outs):
            k = n - 1 - i
            pairs = [(z, z ^ k) for z in range(n)]
            back.append((k, [a], lax.ppermute(out, "tm", pairs) if k else out))
    sums = []
    for a in range(CHUNKS):
        held = [(k, chunks.index(a) * rows, part) for k, chunks, part in back if a in chunks]
        places = [(k, first) for k, first, _ in held]
        parts = [part for _, _, part in held]
        keep, send = pl.pallas_call(
            functools.partial(project_kernel, n, cores, places),
            out_shape=[
                jax.ShapeDtypeStruct((count, model), jnp.float32),
                jax.ShapeDtypeStruct((count, model), bf16),
            ],
            in_specs=[VMEM] * (2 + n),
            out_specs=[VMEM] * 2,
            scratch_shapes=[pltpu.VMEM((n, rows, wide), bf16)],
            compiler_params=pltpu.CompilerParams(vmem_limit_bytes=24 * 2**20),
            name="project",
        )(out_weight, other_weight, *parts)
        sums += [keep, swapped(send, "head")]
    return pl.pallas_call(
        functools.partial(add_kernel, CHUNKS),
        out_shape=jax.ShapeDtypeStruct((1, tokens, model), bf16),
        in_specs=[VMEM] * (2 * CHUNKS),
        out_specs=VMEM,
        compiler_params=pltpu.CompilerParams(vmem_limit_bytes=4 * 2**20),
        name="add",
    )(*sums)


def solution(mesh):
    n, cores, xs = mesh.shape["tm"], mesh.shape["sub"], mesh.shape["head"]

    def local(queries, keys, values, band_table, windows, out_weight):
        frames, length, width = queries.shape
        fits = (
            frames == 1
            and n > 2
            and n & (n - 1) == 0
            and cores == 2
            and xs == 2
            and n % cores == 0
            and width * cores % (n * HEAD) == 0
            and length % (xs * cores * CHUNKS * 16) == 0
        )
        step = functools.partial(spread, n, cores) if fits else gathered
        return step(queries, keys, values, band_table, windows, out_weight)

    return jax.shard_map(
        local,
        mesh=mesh,
        in_specs=(
            P(("clip", "tm"), None, ("head", "sub")),
            P(("clip", "tm"), None, ("head", "sub")),
            P(("clip", "tm"), None, ("head", "sub")),
            P(),
            P(),
            P(("head", "sub"), None),
        ),
        out_specs=P(("clip", "tm"), ("head", "sub"), None),
        check_vma=False,
    )
```

profile of v0, /device:TPU:0, one launch (start us, length us, event | category | flops | bytes accessed | tf_op | source)
XLA Modules:
  0.0 56.8 jit_solution(5726225071454038194)
XLA Ops:
  0.0 1.7 %pack.2 = bf16[3,128,384]{2,1,0:T(8,128)(2,1)} custom-call(bf16[1,256,768]{2,1,0:T(8,128)(2,1)} %q_ref.2, bf16[1,256,768]{2,1,0:T(8,128)(2,1)} %k_ref.2, bf16[1,256,768]{2,1,0:T(8,128)(2,1)} %v_ref.2), custom_call_target="tpu_custom_call" | custom-call | tf_op jit(solution)/shard_map/pack/pallas_call | solution.py:324
  1.7 0.5 collective-permute-start
  2.2 2.6 %collective-permute-start.3 = (bf16[3,128,384]{2,1,0:T(8,128)(2,1)}, bf16[3,128,384]{2,1,0:T(8,128)(2,1)S(1)}, u32[]{:S(2)}, u32[]{:S(2)}) collective-permute-start(bf16[3,128,384]{2,1,0:T(8,128)(2,1)} %pack.2), channel_id=1, source_target_pairs={{0,4},{1,12},{4,5},{5,13},{8,0},{9,8},{12,1},{13,9},{2,6},{3,14},{... | collective-permute-start | bytes 884744 | tf_op jit(solution)/shard_map/ppermute | solution.py:357
  4.9 0.0 copy-start
  4.9 1.0 %copy-done = bf16[1,256,768]{2,1,0:T(8,128)(2,1)S(1)} copy-done((bf16[1,256,768]{2,1,0:T(8,128)(2,1)S(1)}, bf16[1,256,768]{2,1,0:T(8,128)(2,1)}, u32[]{:S(2)}) %copy-start) | copy-done | bytes 393240
  5.9 0.0 copy-start.1
  5.9 1.0 %copy-done.1 = bf16[1,256,768]{2,1,0:T(8,128)(2,1)S(1)} copy-done((bf16[1,256,768]{2,1,0:T(8,128)(2,1)S(1)}, bf16[1,256,768]{2,1,0:T(8,128)(2,1)}, u32[]{:S(2)}) %copy-start.1) | copy-done | bytes 393240
  6.9 0.0 copy-start.2
  6.9 1.0 %copy-done.2 = bf16[1,256,768]{2,1,0:T(8,128)(2,1)S(1)} copy-done((bf16[1,256,768]{2,1,0:T(8,128)(2,1)S(1)}, bf16[1,256,768]{2,1,0:T(8,128)(2,1)}, u32[]{:S(2)}) %copy-start.2) | copy-done | bytes 393240
  7.8 0.3 pack.3
  8.1 2.2 %collective-permute-start.2 = (bf16[3,128,384]{2,1,0:T(8,128)(2,1)S(1)}, bf16[3,128,384]{2,1,0:T(8,128)(2,1)S(1)}, u32[]{:S(2)}, u32[]{:S(2)}) collective-permute-start(bf16[3,128,384]{2,1,0:T(8,128)(2,1)S(1)} %get-tuple-element.38), channel_id=1, source_target_pairs={{0,1},{1,9},{4,0},{5,8},{8,5},{9,13},{12,4},{13,12},{2,3},{3,11},{... | collective-permute-start | bytes 884744 | tf_op jit(solution)/shard_map/ppermute | solution.py:357
  10.3 2.1 %collective-permute-start.4 = (bf16[3,128,384]{2,1,0:T(8,128)(2,1)S(1)}, bf16[3,128,384]{2,1,0:T(8,128)(2,1)S(1)}, u32[]{:S(2)}, u32[]{:S(2)}) collective-permute-start(bf16[3,128,384]{2,1,0:T(8,128)(2,1)S(1)} %get-tuple-element.39), channel_id=1, source_target_pairs={{0,5},{1,13},{4,4},{5,12},{8,1},{9,9},{12,0},{13,8},{2,7},{3,15},{... | collective-permute-start | bytes 884744 | tf_op jit(solution)/shard_map/ppermute | solution.py:357
  12.5 0.0 copy-start.3
  12.5 0.7 %copy-done.3 = s32[4,4]{1,0:T(4,128)S(1)} copy-done((s32[4,4]{1,0:T(4,128)S(1)}, s32[4,4]{1,0:T(4,128)}, u32[]{:S(2)}) %copy-start.3) | copy-done | bytes 88
  13.1 0.0 copy-start.4
  13.1 0.7 %copy-done.4 = s32[7]{0:T(128)S(1)} copy-done((s32[7]{0:T(128)S(1)}, s32[7]{0:T(128)}, u32[]{:S(2)}) %copy-start.4) | copy-done | bytes 52
  13.8 0.7 %bias.1.bias_ref = f32[512,1024]{1,0:T(8,128)S(1)} custom-call(s32[4,4]{1,0:T(4,128)S(1)} %copy-done.3, s32[7]{0:T(128)S(1)} %copy-done.4), custom_call_target="tpu_custom_call" | custom-call | tf_op jit(solution)/shard_map/bias/pallas_call | solution.py:347
  14.5 0.7 %collective-permute-start.1 = (bf16[3,128,384]{2,1,0:T(8,128)(2,1)S(1)}, bf16[3,128,384]{2,1,0:T(8,128)(2,1)S(1)}, u32[]{:S(2)}, u32[]{:S(2)}) collective-permute-start(bf16[3,128,384]{2,1,0:T(8,128)(2,1)S(1)} %get-tuple-element.37), channel_id=1, source_target_pairs={{0,0},{1,8},{4,1},{5,9},{8,4},{9,12},{12,5},{13,13},{2,2},{3,10},{... | collective-permute-start | bytes 884744 | tf_op jit(solution)/shard_map/ppermute | solution.py:357
  15.2 1.9 %collective-permute-done.2.rest_1_ = bf16[3,128,384]{2,1,0:T(8,128)(2,1)S(1)} collective-permute-done((bf16[3,128,384]{2,1,0:T(8,128)(2,1)S(1)}, bf16[3,128,384]{2,1,0:T(8,128)(2,1)S(1)}, u32[]{:S(2)}, u32[]{:S(2)}) %collective-permute-start.2) | collective-permute-done | bytes 294944 | tf_op jit(solution)/shard_map/ppermute | solution.py:357
  17.1 1.9 %collective-permute-start.5 = (bf16[3,128,384]{2,1,0:T(8,128)(2,1)S(1)}, bf16[3,128,384]{2,1,0:T(8,128)(2,1)S(1)}, u32[]{:S(2)}, u32[]{:S(2)}) collective-permute-start(bf16[3,128,384]{2,1,0:T(8,128)(2,1)S(1)} %collective-permute-done.2.rest_1_), channel_id=1, source_target_pairs={{0,1},{1,0},{2,3},{3,2},{4,5},{5,4},{6,7},{7,6},{8,9},{9,8},{10,11... | collective-permute-start | bytes 884744 | tf_op jit(solution)/shard_map/ppermute | solution.py:310
  19.0 0.0 collective-permute-done.3.rest_2_
  19.0 0.1 collective-permute-start.6
  19.1 5.4 %collective-permute-done.4.rest_3_ = bf16[3,128,384]{2,1,0:T(8,128)(2,1)S(1)} collective-permute-done((bf16[3,128,384]{2,1,0:T(8,128)(2,1)S(1)}, bf16[3,128,384]{2,1,0:T(8,128)(2,1)S(1)}, u32[]{:S(2)}, u32[]{:S(2)}) %collective-permute-start.4) | collective-permute-done | bytes 294944 | tf_op jit(solution)/shard_map/ppermute | solution.py:357
  24.5 5.4 %collective-permute-start.7 = (bf16[3,128,384]{2,1,0:T(8,128)(2,1)S(1)}, bf16[3,128,384]{2,1,0:T(8,128)(2,1)S(1)}, u32[]{:S(2)}, u32[]{:S(2)}) collective-permute-start(bf16[3,128,384]{2,1,0:T(8,128)(2,1)S(1)} %collective-permute-done.4.rest_3_), channel_id=1, source_target_pairs={{0,1},{1,0},{2,3},{3,2},{4,5},{5,4},{6,7},{7,6},{8,9},{9,8},{10,11... | collective-permute-start | bytes 884744 | tf_op jit(solution)/shard_map/ppermute | solution.py:310
  29.9 0.0 collective-permute-done.1.rest_0_
  29.9 0.0 collective-permute-start.8
  29.9 0.0 collective-permute-done.other_w
  29.9 0.0 collective-permute-done.5.rest_4_
  29.9 0.0 collective-permute-done.6.rest_5_
  29.9 1.2 %collective-permute-done.7.rest_6_ = bf16[3,128,384]{2,1,0:T(8,128)(2,1)S(1)} collective-permute-done((bf16[3,128,384]{2,1,0:T(8,128)(2,1)S(1)}, bf16[3,128,384]{2,1,0:T(8,128)(2,1)S(1)}, u32[]{:S(2)}, u32[]{:S(2)}) %collective-permute-start.7) | collective-permute-done | bytes 294944 | tf_op jit(solution)/shard_map/ppermute | solution.py:310
  31.1 0.0 slice-start
  31.1 2.4 %attend_early.1 = (f32[3,512,128]{2,1,0:T(8,128)S(1)}, f32[3,512,128]{2,1,0:T(8,128)S(1)}, f32[3,512,128]{2,1,0:T(8,128)S(1)}) custom-call(f32[512,1024]{1,0:T(8,128)S(1)} %bias.1.bias_ref, bf16[3,128,384]{2,1,0:T(8,128)(2,1)S(1)} %collective-permute-done.1.rest_0_, bf16[3,128,384]{2,1,0:T(8,128)(2,1)S(1)} %collective-permute-done.2.rest_1_, ...), custom_call_target="tpu_custom_call" | custom-call | tf_op jit(solution)/shard_map/attend_early/pallas_call | solution.py:367
  33.6 0.0 collective-permute-done.8.rest_4_
  33.6 0.0 slice-start.1
  33.6 0.6 %attend_late.2 = (bf16[64,384]{1,0:T(8,128)(2,1)S(1)}, bf16[64,384]{1,0:T(8,128)(2,1)S(1)}, bf16[64,384]{1,0:T(8,128)(2,1)S(1)}, bf16[64,384]{1,0:T(8,128)(2,1)S(1)}) custom-call(f32[512,1024]{1,0:T(8,128)S(1)} %bias.1.bias_ref, f32[3,512,128]{2,1,0:T(8,128)S(1)} %get-tuple-element.40.numer_ref, f32[3,512,128]{2,1,0:T(8,128)S(1)} %get-tuple-element.41.total_ref, ...), custom_call_target="tpu_custom_call" | custom-call | tf_op jit(solution)/shard_map/attend_late/pallas_call | solution.py:382
  34.2 3.7 %collective-permute-start.9 = (bf16[64,384]{1,0:T(8,128)(2,1)S(1)}, bf16[64,384]{1,0:T(8,128)(2,1)S(1)}, u32[]{:S(2)}, u32[]{:S(2)}) collective-permute-start(bf16[64,384]{1,0:T(8,128)(2,1)S(1)} %get-tuple-element.43), channel_id=1, source_target_pairs={{0,12},{4,8},{8,4},{12,0},{1,13},{5,9},{9,5},{13,1},{2,14},{6,10},... | collective-permute-start | bytes 147464 | tf_op jit(solution)/shard_map/ppermute | solution.py:399
  38.0 0.6 %collective-permute-start.10 = (bf16[64,384]{1,0:T(8,128)(2,1)S(1)}, bf16[64,384]{1,0:T(8,128)(2,1)S(1)}, u32[]{:S(2)}, u32[]{:S(2)}) collective-permute-start(bf16[64,384]{1,0:T(8,128)(2,1)S(1)} %get-tuple-element.44), channel_id=1, source_target_pairs={{0,8},{4,12},{8,0},{12,4},{1,9},{5,13},{9,1},{13,5},{2,10},{6,14},... | collective-permute-start | bytes 147464 | tf_op jit(solution)/shard_map/ppermute | solution.py:399
  38.6 0.5 collective-permute-start.11
  39.1 0.6 %attend_late.3 = (bf16[64,384]{1,0:T(8,128)(2,1)S(1)}, bf16[64,384]{1,0:T(8,128)(2,1)S(1)}, bf16[64,384]{1,0:T(8,128)(2,1)S(1)}, bf16[64,384]{1,0:T(8,128)(2,1)S(1)}) custom-call(f32[512,1024]{1,0:T(8,128)S(1)} %bias.1.bias_ref, f32[3,512,128]{2,1,0:T(8,128)S(1)} %get-tuple-element.40.numer_ref, f32[3,512,128]{2,1,0:T(8,128)S(1)} %get-tuple-element.41.total_ref, ...), custom_call_target="tpu_custom_call" | custom-call | tf_op jit(solution)/shard_map/attend_late/pallas_call | solution.py:382
  39.7 3.3 %collective-permute-start.13 = (bf16[64,384]{1,0:T(8,128)(2,1)S(1)}, bf16[64,384]{1,0:T(8,128)(2,1)S(1)}, u32[]{:S(2)}, u32[]{:S(2)}) collective-permute-start(bf16[64,384]{1,0:T(8,128)(2,1)S(1)} %get-tuple-element.49), channel_id=1, source_target_pairs={{0,12},{4,8},{8,4},{12,0},{1,13},{5,9},{9,5},{13,1},{2,14},{6,10},... | collective-permute-start | bytes 147464 | tf_op jit(solution)/shard_map/ppermute | solution.py:399
  43.0 0.0 collective-permute-start.14
  43.0 0.0 collective-permute-done.9.rest_0_
  43.0 1.1 %collective-permute-start.15 = (bf16[64,384]{1,0:T(8,128)(2,1)S(1)}, bf16[64,384]{1,0:T(8,128)(2,1)S(1)}, u32[]{:S(2)}, u32[]{:S(2)}) collective-permute-start(bf16[64,384]{1,0:T(8,128)(2,1)S(1)} %get-tuple-element.51), channel_id=1, source_target_pairs={{0,4},{4,0},{8,12},{12,8},{1,5},{5,1},{9,13},{13,9},{2,6},{6,2},{1... | collective-permute-start | bytes 147464 | tf_op jit(solution)/shard_map/ppermute | solution.py:399
  44.2 0.0 collective-permute-done.10.rest_1_
  44.2 0.0 collective-permute-done.11.rest_2_
  44.2 0.0 slice-done
  44.2 0.0 slice-done.1
  44.2 1.8 %project.2 = (f32[32,3072]{1,0:T(8,128)S(1)}, bf16[32,3072]{1,0:T(8,128)(2,1)S(1)}) custom-call(bf16[768,3072]{1,0:T(8,128)(2,1)S(1)} %bitcast.1, bf16[768,3072]{1,0:T(8,128)(2,1)S(1)} %collective-permute-done.other_w, bf16[64,384]{1,0:T(8,128)(2,1)S(1)} %collective-permute-done.9.rest_0_, bf16[64,384]{1,0:T(8,128)(2,1)S(1)} %collective-permute-done.10.rest_1_, ...), custom_call_target="tpu_custom_call" | custom-call | tf_op jit(solution)/shard_map/project/pallas_call | solution.py:405
  46.0 1.6 %collective-permute-start.12 = (bf16[32,3072]{1,0:T(8,128)(2,1)S(1)}, bf16[32,3072]{1,0:T(8,128)(2,1)S(1)}, u32[]{:S(2)}, u32[]{:S(2)}) collective-permute-start(bf16[32,3072]{1,0:T(8,128)(2,1)S(1)} %get-tuple-element.48), channel_id=1, source_target_pairs={{0,2},{2,0},{1,3},{3,1},{4,6},{6,4},{5,7},{7,5},{8,10},{10,8},{9,1... | collective-permute-start | bytes 589832 | tf_op jit(solution)/shard_map/ppermute | solution.py:310
  47.5 0.0 collective-permute-done.13.rest_0_
  47.5 0.8 %collective-permute-done.14.rest_1_ = bf16[64,384]{1,0:T(8,128)(2,1)S(1)} collective-permute-done((bf16[64,384]{1,0:T(8,128)(2,1)S(1)}, bf16[64,384]{1,0:T(8,128)(2,1)S(1)}, u32[]{:S(2)}, u32[]{:S(2)}) %collective-permute-start.14) | collective-permute-done | bytes 49184 | tf_op jit(solution)/shard_map/ppermute | solution.py:399
  48.3 0.0 collective-permute-done.15.rest_2_
  48.3 1.8 %project.3 = (f32[32,3072]{1,0:T(8,128)S(1)}, bf16[32,3072]{1,0:T(8,128)(2,1)S(1)}) custom-call(bf16[768,3072]{1,0:T(8,128)(2,1)S(1)} %bitcast.1, bf16[768,3072]{1,0:T(8,128)(2,1)S(1)} %collective-permute-done.other_w, bf16[64,384]{1,0:T(8,128)(2,1)S(1)} %collective-permute-done.13.rest_0_, bf16[64,384]{1,0:T(8,128)(2,1)S(1)} %collective-permute-done.14.rest_1_, ...), custom_call_target="tpu_custom_call" | custom-call | tf_op jit(solution)/shard_map/project/pallas_call | solution.py:405
  50.1 1.6 %collective-permute-start.16 = (bf16[32,3072]{1,0:T(8,128)(2,1)S(1)}, bf16[32,3072]{1,0:T(8,128)(2,1)S(1)}, u32[]{:S(2)}, u32[]{:S(2)}) collective-permute-start(bf16[32,3072]{1,0:T(8,128)(2,1)S(1)} %get-tuple-element.54), channel_id=1, source_target_pairs={{0,2},{2,0},{1,3},{3,1},{4,6},{6,4},{5,7},{7,5},{8,10},{10,8},{9,1... | collective-permute-start | bytes 589832 | tf_op jit(solution)/shard_map/ppermute | solution.py:310
  51.7 0.8 %collective-permute-done.12.refs_1_ = bf16[32,3072]{1,0:T(8,128)(2,1)S(1)} collective-permute-done((bf16[32,3072]{1,0:T(8,128)(2,1)S(1)}, bf16[32,3072]{1,0:T(8,128)(2,1)S(1)}, u32[]{:S(2)}, u32[]{:S(2)}) %collective-permute-start.12) | collective-permute-done | bytes 196640 | tf_op jit(solution)/shard_map/ppermute | solution.py:310
  52.5 3.5 %collective-permute-done.16.refs_3_ = bf16[32,3072]{1,0:T(8,128)(2,1)S(1)} collective-permute-done((bf16[32,3072]{1,0:T(8,128)(2,1)S(1)}, bf16[32,3072]{1,0:T(8,128)(2,1)S(1)}, u32[]{:S(2)}, u32[]{:S(2)}) %collective-permute-start.16) | collective-permute-done | bytes 196640 | tf_op jit(solution)/shard_map/ppermute | solution.py:310
  55.9 0.8 %add.1 = bf16[1,64,3072]{2,1,0:T(8,128)(2,1)} custom-call(f32[32,3072]{1,0:T(8,128)S(1)} %get-tuple-element.47.refs_0_, bf16[32,3072]{1,0:T(8,128)(2,1)S(1)} %collective-permute-done.12.refs_1_, f32[32,3072]{1,0:T(8,128)S(1)} %get-tuple-element.53.refs_2_, bf16[32,3072]{1,0:T(8,128)(2,1)S(1)} %collective-permute-done.16.refs_3_), custom_call_target="tpu_custom_call" | custom-call | tf_op jit(solution)/shard_map/add/pallas_call | solution.py:418
  (1 shorter events, 0.0 us)
Async XLA Ops:
  1.7 28.2 %collective-permute-start = (bf16[768,3072]{1,0:T(8,128)(2,1)}, bf16[768,3072]{1,0:T(8,128)(2,1)S(1)}, u32[]{:S(2)}, u32[]{:S(2)}) collective-permute-start(bf16[768,3072]{1,0:T(8,128)(2,1)} %own_w.3), channel_id=1, source_target_pairs={{0,1},{1,0},{2,3},{3,2},{4,5},{5,4},{6,7},{7,6},{8,9},{9,8},{10,11... | collective-permute-start | bytes 14155784 | tf_op jit(solution)/shard_map/ppermute | solution.py:310
  2.2 16.8 %collective-permute-start.3 = (bf16[3,128,384]{2,1,0:T(8,128)(2,1)}, bf16[3,128,384]{2,1,0:T(8,128)(2,1)S(1)}, u32[]{:S(2)}, u32[]{:S(2)}) collective-permute-start(bf16[3,128,384]{2,1,0:T(8,128)(2,1)} %pack.2), channel_id=1, source_target_pairs={{0,4},{1,12},{4,5},{5,13},{8,0},{9,8},{12,1},{13,9},{2,6},{3,14},{... | collective-permute-start | bytes 884744 | tf_op jit(solution)/shard_map/ppermute | solution.py:357
  4.9 1.0 %copy-start = (bf16[1,256,768]{2,1,0:T(8,128)(2,1)S(1)}, bf16[1,256,768]{2,1,0:T(8,128)(2,1)}, u32[]{:S(2)}) copy-start(bf16[1,256,768]{2,1,0:T(8,128)(2,1)} %q_ref.2) | copy-start | bytes 1179652
  5.9 1.0 %copy-start.1 = (bf16[1,256,768]{2,1,0:T(8,128)(2,1)S(1)}, bf16[1,256,768]{2,1,0:T(8,128)(2,1)}, u32[]{:S(2)}) copy-start(bf16[1,256,768]{2,1,0:T(8,128)(2,1)} %k_ref.2) | copy-start | bytes 1179652
  6.9 1.0 %copy-start.2 = (bf16[1,256,768]{2,1,0:T(8,128)(2,1)S(1)}, bf16[1,256,768]{2,1,0:T(8,128)(2,1)}, u32[]{:S(2)}) copy-start(bf16[1,256,768]{2,1,0:T(8,128)(2,1)} %v_ref.2) | copy-start | bytes 1179652
  8.1 9.0 %collective-permute-start.2 = (bf16[3,128,384]{2,1,0:T(8,128)(2,1)S(1)}, bf16[3,128,384]{2,1,0:T(8,128)(2,1)S(1)}, u32[]{:S(2)}, u32[]{:S(2)}) collective-permute-start(bf16[3,128,384]{2,1,0:T(8,128)(2,1)S(1)} %get-tuple-element.38), channel_id=1, source_target_pairs={{0,1},{1,9},{4,0},{5,8},{8,5},{9,13},{12,4},{13,12},{2,3},{3,11},{... | collective-permute-start | bytes 884744 | tf_op jit(solution)/shard_map/ppermute | solution.py:357
  10.3 14.1 %collective-permute-start.4 = (bf16[3,128,384]{2,1,0:T(8,128)(2,1)S(1)}, bf16[3,128,384]{2,1,0:T(8,128)(2,1)S(1)}, u32[]{:S(2)}, u32[]{:S(2)}) collective-permute-start(bf16[3,128,384]{2,1,0:T(8,128)(2,1)S(1)} %get-tuple-element.39), channel_id=1, source_target_pairs={{0,5},{1,13},{4,4},{5,12},{8,1},{9,9},{12,0},{13,8},{2,7},{3,15},{... | collective-permute-start | bytes 884744 | tf_op jit(solution)/shard_map/ppermute | solution.py:357
  12.5 0.7 %copy-start.3 = (s32[4,4]{1,0:T(4,128)S(1)}, s32[4,4]{1,0:T(4,128)}, u32[]{:S(2)}) copy-start(s32[4,4]{1,0:T(4,128)} %band_ref.1) | copy-start | bytes 196
  13.1 0.7 %copy-start.4 = (s32[7]{0:T(128)S(1)}, s32[7]{0:T(128)}, u32[]{:S(2)}) copy-start(s32[7]{0:T(128)} %reach_ref.1) | copy-start | bytes 88
  14.5 15.4 %collective-permute-start.1 = (bf16[3,128,384]{2,1,0:T(8,128)(2,1)S(1)}, bf16[3,128,384]{2,1,0:T(8,128)(2,1)S(1)}, u32[]{:S(2)}, u32[]{:S(2)}) collective-permute-start(bf16[3,128,384]{2,1,0:T(8,128)(2,1)S(1)} %get-tuple-element.37), channel_id=1, source_target_pairs={{0,0},{1,8},{4,1},{5,9},{8,4},{9,12},{12,5},{13,13},{2,2},{3,10},{... | collective-permute-start | bytes 884744 | tf_op jit(solution)/shard_map/ppermute | solution.py:357
  17.1 12.8 %collective-permute-start.5 = (bf16[3,128,384]{2,1,0:T(8,128)(2,1)S(1)}, bf16[3,128,384]{2,1,0:T(8,128)(2,1)S(1)}, u32[]{:S(2)}, u32[]{:S(2)}) collective-permute-start(bf16[3,128,384]{2,1,0:T(8,128)(2,1)S(1)} %collective-permute-done.2.rest_1_), channel_id=1, source_target_pairs={{0,1},{1,0},{2,3},{3,2},{4,5},{5,4},{6,7},{7,6},{8,9},{9,8},{10,11... | collective-permute-start | bytes 884744 | tf_op jit(solution)/shard_map/ppermute | solution.py:310
  19.0 11.0 %collective-permute-start.6 = (bf16[3,128,384]{2,1,0:T(8,128)(2,1)S(1)}, bf16[3,128,384]{2,1,0:T(8,128)(2,1)S(1)}, u32[]{:S(2)}, u32[]{:S(2)}) collective-permute-start(bf16[3,128,384]{2,1,0:T(8,128)(2,1)S(1)} %collective-permute-done.3.rest_2_), channel_id=1, source_target_pairs={{0,1},{1,0},{2,3},{3,2},{4,5},{5,4},{6,7},{7,6},{8,9},{9,8},{10,11... | collective-permute-start | bytes 884744 | tf_op jit(solution)/shard_map/ppermute | solution.py:310
  24.5 6.7 %collective-permute-start.7 = (bf16[3,128,384]{2,1,0:T(8,128)(2,1)S(1)}, bf16[3,128,384]{2,1,0:T(8,128)(2,1)S(1)}, u32[]{:S(2)}, u32[]{:S(2)}) collective-permute-start(bf16[3,128,384]{2,1,0:T(8,128)(2,1)S(1)} %collective-permute-done.4.rest_3_), channel_id=1, source_target_pairs={{0,1},{1,0},{2,3},{3,2},{4,5},{5,4},{6,7},{7,6},{8,9},{9,8},{10,11... | collective-permute-start | bytes 884744 | tf_op jit(solution)/shard_map/ppermute | solution.py:310
  29.9 3.7 %collective-permute-start.8 = (bf16[3,128,384]{2,1,0:T(8,128)(2,1)S(1)}, bf16[3,128,384]{2,1,0:T(8,128)(2,1)S(1)}, u32[]{:S(2)}, u32[]{:S(2)}) collective-permute-start(bf16[3,128,384]{2,1,0:T(8,128)(2,1)S(1)} %collective-permute-done.1.rest_0_), channel_id=1, source_target_pairs={{0,1},{1,0},{2,3},{3,2},{4,5},{5,4},{6,7},{7,6},{8,9},{9,8},{10,11... | collective-permute-start | bytes 884744 | tf_op jit(solution)/shard_map/ppermute | solution.py:310
  31.1 13.0 %slice-start = ((s8[4718592]{0:T(1024)(128)(4,1)}), s8[4194304]{0:T(1024)(128)(4,1)S(1)}, s32[]{:S(2)}) async-start(s8[4718592]{0:T(1024)(128)(4,1)} %bitcast), calls=%async_computation | async-start | bytes 8388608
  33.6 10.6 %slice-start.1 = ((s8[4718592]{0:T(1024)(128)(4,1)}), s8[524288]{0:T(1024)(128)(4,1)S(1)}, s32[]{:S(2)}) async-start(s8[4718592]{0:T(1024)(128)(4,1)} %bitcast), calls=%async_computation.1 | async-start | bytes 1048576
  34.2 8.8 %collective-permute-start.9 = (bf16[64,384]{1,0:T(8,128)(2,1)S(1)}, bf16[64,384]{1,0:T(8,128)(2,1)S(1)}, u32[]{:S(2)}, u32[]{:S(2)}) collective-permute-start(bf16[64,384]{1,0:T(8,128)(2,1)S(1)} %get-tuple-element.43), channel_id=1, source_target_pairs={{0,12},{4,8},{8,4},{12,0},{1,13},{5,9},{9,5},{13,1},{2,14},{6,10},... | collective-permute-start | bytes 147464 | tf_op jit(solution)/shard_map/ppermute | solution.py:399
  38.0 6.2 %collective-permute-start.10 = (bf16[64,384]{1,0:T(8,128)(2,1)S(1)}, bf16[64,384]{1,0:T(8,128)(2,1)S(1)}, u32[]{:S(2)}, u32[]{:S(2)}) collective-permute-start(bf16[64,384]{1,0:T(8,128)(2,1)S(1)} %get-tuple-element.44), channel_id=1, source_target_pairs={{0,8},{4,12},{8,0},{12,4},{1,9},{5,13},{9,1},{13,5},{2,10},{6,14},... | collective-permute-start | bytes 147464 | tf_op jit(solution)/shard_map/ppermute | solution.py:399
  38.6 5.6 %collective-permute-start.11 = (bf16[64,384]{1,0:T(8,128)(2,1)S(1)}, bf16[64,384]{1,0:T(8,128)(2,1)S(1)}, u32[]{:S(2)}, u32[]{:S(2)}) collective-permute-start(bf16[64,384]{1,0:T(8,128)(2,1)S(1)} %get-tuple-element.45), channel_id=1, source_target_pairs={{0,4},{4,0},{8,12},{12,8},{1,5},{5,1},{9,13},{13,9},{2,6},{6,2},{1... | collective-permute-start | bytes 147464 | tf_op jit(solution)/shard_map/ppermute | solution.py:399
  39.7 7.8 %collective-permute-start.13 = (bf16[64,384]{1,0:T(8,128)(2,1)S(1)}, bf16[64,384]{1,0:T(8,128)(2,1)S(1)}, u32[]{:S(2)}, u32[]{:S(2)}) collective-permute-start(bf16[64,384]{1,0:T(8,128)(2,1)S(1)} %get-tuple-element.49), channel_id=1, source_target_pairs={{0,12},{4,8},{8,4},{12,0},{1,13},{5,9},{9,5},{13,1},{2,14},{6,10},... | collective-permute-start | bytes 147464 | tf_op jit(solution)/shard_map/ppermute | solution.py:399
  43.0 5.3 %collective-permute-start.14 = (bf16[64,384]{1,0:T(8,128)(2,1)S(1)}, bf16[64,384]{1,0:T(8,128)(2,1)S(1)}, u32[]{:S(2)}, u32[]{:S(2)}) collective-permute-start(bf16[64,384]{1,0:T(8,128)(2,1)S(1)} %get-tuple-element.50), channel_id=1, source_target_pairs={{0,8},{4,12},{8,0},{12,4},{1,9},{5,13},{9,1},{13,5},{2,10},{6,14},... | collective-permute-start | bytes 147464 | tf_op jit(solution)/shard_map/ppermute | solution.py:399
  43.0 5.3 %collective-permute-start.15 = (bf16[64,384]{1,0:T(8,128)(2,1)S(1)}, bf16[64,384]{1,0:T(8,128)(2,1)S(1)}, u32[]{:S(2)}, u32[]{:S(2)}) collective-permute-start(bf16[64,384]{1,0:T(8,128)(2,1)S(1)} %get-tuple-element.51), channel_id=1, source_target_pairs={{0,4},{4,0},{8,12},{12,8},{1,5},{5,1},{9,13},{13,9},{2,6},{6,2},{1... | collective-permute-start | bytes 147464 | tf_op jit(solution)/shard_map/ppermute | solution.py:399
  46.0 6.5 %collective-permute-start.12 = (bf16[32,3072]{1,0:T(8,128)(2,1)S(1)}, bf16[32,3072]{1,0:T(8,128)(2,1)S(1)}, u32[]{:S(2)}, u32[]{:S(2)}) collective-permute-start(bf16[32,3072]{1,0:T(8,128)(2,1)S(1)} %get-tuple-element.48), channel_id=1, source_target_pairs={{0,2},{2,0},{1,3},{3,1},{4,6},{6,4},{5,7},{7,5},{8,10},{10,8},{9,1... | collective-permute-start | bytes 589832 | tf_op jit(solution)/shard_map/ppermute | solution.py:310
  50.1 5.8 %collective-permute-start.16 = (bf16[32,3072]{1,0:T(8,128)(2,1)S(1)}, bf16[32,3072]{1,0:T(8,128)(2,1)S(1)}, u32[]{:S(2)}, u32[]{:S(2)}) collective-permute-start(bf16[32,3072]{1,0:T(8,128)(2,1)S(1)} %get-tuple-element.54), channel_id=1, source_target_pairs={{0,2},{2,0},{1,3},{3,1},{4,6},{6,4},{5,7},{7,5},{8,10},{10,8},{9,1... | collective-permute-start | bytes 589832 | tf_op jit(solution)/shard_map/ppermute | solution.py:310
where the time goes:
time: 57.1 us; the launch traced here: 56.8 us
  starting transfers between devices  28 us (49%)
  waiting for transfers between devices  13.5 us (24%)
  Pallas kernels  10.8 us (19%)
  local copies, waits for them, and re-layouts  4.33 us (8%)
    ppermute x7, starting transfers between devices, swapped(): return lax.ppermute(x, axis, [(0, 1), (1, 0)])  11 us
    ppermute x6, starting transfers between devices, spread(): back.append((k, [a], lax.ppermute(out, 'tm', pairs) if k else out))  9.27 us
    ppermute x4, starting transfers between devices, spread(): own = [lax.ppermute(blocks[r], ('tm', 'sub'), rounds[r]) for r in range(n)]  7.65 us
    ppermute x4, waiting for transfers between devices, spread(): own = [lax.ppermute(blocks[r], ('tm', 'sub'), rounds[r]) for r in range(n)]  7.28 us
    ppermute x7, waiting for transfers between devices, swapped(): return lax.ppermute(x, axis, [(0, 1), (1, 0)])  5.44 us
    unnamed x14, local copies, waits for them, and re-layouts  4.33 us
    pallas_call x2, Pallas kernels, spread(): pl.pallas_call(functools.partial(project_kernel, n, cores, places), out_s...  3.59 us
    pallas_call x1, Pallas kernels, spread(): pl.pallas_call(functools.partial(attend_early_kernel, n, cores, tokens),...  2.44 us
  transfers between devices with their start and end apart: 17, of which 6 were waited for; matrix products, arithmetic and copies ran while one was open for 0% of the time, Pallas kernels for 13%

commit v1 on v0

--- a/solution.py
+++ b/solution.py
@@ -296,14 +296,11 @@
     keep_ref[...] = total[count:]
 
 
-def add_kernel(chunks, *refs):
-    out_ref = refs[-1]
-    for a in range(chunks):
-        keep, got = refs[2 * a], refs[2 * a + 1]
-        count = keep.shape[0]
-        out_ref[0, a * count : (a + 1) * count] = (
-            keep[...] + got[...].astype(jnp.float32)
-        ).astype(out_ref.dtype)
+def add_kernel(first, keep_ref, got_ref, *rest):
+    out_ref, sum_ref, sem = rest[-3:]
+    count = keep_ref.shape[0]
+    sum_ref[...] = (keep_ref[...] + got_ref[...].astype(jnp.float32)).astype(sum_ref.dtype)
+    run_copies([(sum_ref, out_ref.at[0, pl.ds(first, count)])], sem)
 
 
 def swapped(x, axis):
@@ -415,14 +412,24 @@
             name="project",
         )(out_weight, other_weight, *parts)
         sums += [keep, swapped(send, "head")]
-    return pl.pallas_call(
-        functools.partial(add_kernel, CHUNKS),
-        out_shape=jax.ShapeDtypeStruct((1, tokens, model), bf16),
-        in_specs=[VMEM] * (2 * CHUNKS),
-        out_specs=VMEM,
-        compiler_params=pltpu.CompilerParams(vmem_limit_bytes=4 * 2**20),
-        name="add",
-    )(*sums)
+    mixed = []
+    for a in range(CHUNKS):
+        mixed = [
+            pl.pallas_call(
+                functools.partial(add_kernel, a * count),
+                out_shape=jax.ShapeDtypeStruct((1, tokens, model), bf16),
+                in_specs=[VMEM] * 2 + [ANY] * len(mixed),
+                out_specs=ANY,
+                scratch_shapes=[
+                    pltpu.VMEM((count, model), bf16),
+                    pltpu.SemaphoreType.DMA((1,)),
+                ],
+                input_output_aliases={2: 0} if mixed else {},
+                compiler_params=pltpu.CompilerParams(vmem_limit_bytes=4 * 2**20),
+                name="add",
+            )(*sums[2 * a : 2 * a + 2], *mixed)
+        ]
+    return mixed[0]
 
 
 def solution(mesh):

time: 57.1 us -> 57 us (level)
  waiting for transfers between devices: 13.5 us -> 12.8 us
  Pallas kernels: 10.8 us -> 11.4 us
    ppermute x7, waiting for transfers between devices: 5.44 us -> 4.71 us  [swapped(): return lax.ppermute(x, axis, [(0, 1), (1, 0)])]
    pallas_call x1 -> x2, Pallas kernels: 0.81 us -> 1.44 us  [spread(): pl.pallas_call(functools.partial(add_kernel, a * count), out_shape=jax.Sh...]
  transfers between devices with their start and end apart: 17 -> 17, of which waited for: 6 -> 6; matrix products, arithmetic and copies ran while one was open for 0% -> 0% of each run, Pallas kernels for 13% -> 15%
where the time goes in v1:
time: 57 us; the launch traced here: 56.7 us
  starting transfers between devices  28 us (49%)
  waiting for transfers between devices  12.8 us (22%)
  Pallas kernels  11.4 us (20%)
  local copies, waits for them, and re-layouts  4.33 us (8%)
    ppermute x7, starting transfers between devices, swapped(): return lax.ppermute(x, axis, [(0, 1), (1, 0)])  11 us
    ppermute x6, starting transfers between devices, spread(): back.append((k, [a], lax.ppermute(out, 'tm', pairs) if k else out))  9.27 us
    ppermute x4, starting transfers between devices, spread(): own = [lax.ppermute(blocks[r], ('tm', 'sub'), rounds[r]) for r in range(n)]  7.65 us
    ppermute x4, waiting for transfers between devices, spread(): own = [lax.ppermute(blocks[r], ('tm', 'sub'), rounds[r]) for r in range(n)]  7.28 us
    ppermute x7, waiting for transfers between devices, swapped(): return lax.ppermute(x, axis, [(0, 1), (1, 0)])  4.71 us
    unnamed x14, local copies, waits for them, and re-layouts  4.33 us
    pallas_call x2, Pallas kernels, spread(): pl.pallas_call(functools.partial(project_kernel, n, cores, places), out_s...  3.59 us
    pallas_call x1, Pallas kernels, spread(): pl.pallas_call(functools.partial(attend_early_kernel, n, cores, tokens),...  2.44 us
  transfers between devices with their start and end apart: 17, of which 6 were waited for; matrix products, arithmetic and copies ran while one was open for 0% of the time, Pallas kernels for 15%

profile of v1, /device:TPU:0, one launch (start us, length us, event | category | flops | bytes accessed | tf_op | source)
XLA Modules:
  0.0 56.7 jit_solution(7195313523350087209)
XLA Ops:
  0.0 1.7 %pack.2 = bf16[3,128,384]{2,1,0:T(8,128)(2,1)} custom-call(bf16[1,256,768]{2,1,0:T(8,128)(2,1)} %q_ref.2, bf16[1,256,768]{2,1,0:T(8,128)(2,1)} %k_ref.2, bf16[1,256,768]{2,1,0:T(8,128)(2,1)} %v_ref.2), custom_call_target="tpu_custom_call" | custom-call | tf_op jit(solution)/shard_map/pack/pallas_call | solution.py:321
  1.7 0.5 collective-permute-start
  2.2 2.6 %collective-permute-start.3 = (bf16[3,128,384]{2,1,0:T(8,128)(2,1)}, bf16[3,128,384]{2,1,0:T(8,128)(2,1)S(1)}, u32[]{:S(2)}, u32[]{:S(2)}) collective-permute-start(bf16[3,128,384]{2,1,0:T(8,128)(2,1)} %pack.2), channel_id=1, source_target_pairs={{0,4},{1,12},{4,5},{5,13},{8,0},{9,8},{12,1},{13,9},{2,6},{3,14},{... | collective-permute-start | bytes 884744 | tf_op jit(solution)/shard_map/ppermute | solution.py:354
  4.9 0.0 copy-start
  4.9 1.0 %copy-done = bf16[1,256,768]{2,1,0:T(8,128)(2,1)S(1)} copy-done((bf16[1,256,768]{2,1,0:T(8,128)(2,1)S(1)}, bf16[1,256,768]{2,1,0:T(8,128)(2,1)}, u32[]{:S(2)}) %copy-start) | copy-done | bytes 393240
  5.9 0.0 copy-start.1
  5.9 1.0 %copy-done.1 = bf16[1,256,768]{2,1,0:T(8,128)(2,1)S(1)} copy-done((bf16[1,256,768]{2,1,0:T(8,128)(2,1)S(1)}, bf16[1,256,768]{2,1,0:T(8,128)(2,1)}, u32[]{:S(2)}) %copy-start.1) | copy-done | bytes 393240
  6.9 0.0 copy-start.2
  6.9 1.0 %copy-done.2 = bf16[1,256,768]{2,1,0:T(8,128)(2,1)S(1)} copy-done((bf16[1,256,768]{2,1,0:T(8,128)(2,1)S(1)}, bf16[1,256,768]{2,1,0:T(8,128)(2,1)}, u32[]{:S(2)}) %copy-start.2) | copy-done | bytes 393240
  7.8 0.3 pack.3
  8.1 2.2 %collective-permute-start.2 = (bf16[3,128,384]{2,1,0:T(8,128)(2,1)S(1)}, bf16[3,128,384]{2,1,0:T(8,128)(2,1)S(1)}, u32[]{:S(2)}, u32[]{:S(2)}) collective-permute-start(bf16[3,128,384]{2,1,0:T(8,128)(2,1)S(1)} %get-tuple-element.38), channel_id=1, source_target_pairs={{0,1},{1,9},{4,0},{5,8},{8,5},{9,13},{12,4},{13,12},{2,3},{3,11},{... | collective-permute-start | bytes 884744 | tf_op jit(solution)/shard_map/ppermute | solution.py:354
  10.3 2.1 %collective-permute-start.4 = (bf16[3,128,384]{2,1,0:T(8,128)(2,1)S(1)}, bf16[3,128,384]{2,1,0:T(8,128)(2,1)S(1)}, u32[]{:S(2)}, u32[]{:S(2)}) collective-permute-start(bf16[3,128,384]{2,1,0:T(8,128)(2,1)S(1)} %get-tuple-element.39), channel_id=1, source_target_pairs={{0,5},{1,13},{4,4},{5,12},{8,1},{9,9},{12,0},{13,8},{2,7},{3,15},{... | collective-permute-start | bytes 884744 | tf_op jit(solution)/shard_map/ppermute | solution.py:354
  12.5 0.0 copy-start.3
  12.5 0.7 %copy-done.3 = s32[4,4]{1,0:T(4,128)S(1)} copy-done((s32[4,4]{1,0:T(4,128)S(1)}, s32[4,4]{1,0:T(4,128)}, u32[]{:S(2)}) %copy-start.3) | copy-done | bytes 88
  13.1 0.0 copy-start.4
  13.1 0.7 %copy-done.4 = s32[7]{0:T(128)S(1)} copy-done((s32[7]{0:T(128)S(1)}, s32[7]{0:T(128)}, u32[]{:S(2)}) %copy-start.4) | copy-done | bytes 52
  13.8 0.7 %bias.1.bias_ref = f32[512,1024]{1,0:T(8,128)S(1)} custom-call(s32[4,4]{1,0:T(4,128)S(1)} %copy-done.3, s32[7]{0:T(128)S(1)} %copy-done.4), custom_call_target="tpu_custom_call" | custom-call | tf_op jit(solution)/shard_map/bias/pallas_call | solution.py:344
  14.5 0.7 %collective-permute-start.1 = (bf16[3,128,384]{2,1,0:T(8,128)(2,1)S(1)}, bf16[3,128,384]{2,1,0:T(8,128)(2,1)S(1)}, u32[]{:S(2)}, u32[]{:S(2)}) collective-permute-start(bf16[3,128,384]{2,1,0:T(8,128)(2,1)S(1)} %get-tuple-element.37), channel_id=1, source_target_pairs={{0,0},{1,8},{4,1},{5,9},{8,4},{9,12},{12,5},{13,13},{2,2},{3,10},{... | collective-permute-start | bytes 884744 | tf_op jit(solution)/shard_map/ppermute | solution.py:354
  15.2 1.9 %collective-permute-done.2.rest_1_ = bf16[3,128,384]{2,1,0:T(8,128)(2,1)S(1)} collective-permute-done((bf16[3,128,384]{2,1,0:T(8,128)(2,1)S(1)}, bf16[3,128,384]{2,1,0:T(8,128)(2,1)S(1)}, u32[]{:S(2)}, u32[]{:S(2)}) %collective-permute-start.2) | collective-permute-done | bytes 294944 | tf_op jit(solution)/shard_map/ppermute | solution.py:354
  17.1 1.9 %collective-permute-start.5 = (bf16[3,128,384]{2,1,0:T(8,128)(2,1)S(1)}, bf16[3,128,384]{2,1,0:T(8,128)(2,1)S(1)}, u32[]{:S(2)}, u32[]{:S(2)}) collective-permute-start(bf16[3,128,384]{2,1,0:T(8,128)(2,1)S(1)} %collective-permute-done.2.rest_1_), channel_id=1, source_target_pairs={{0,1},{1,0},{2,3},{3,2},{4,5},{5,4},{6,7},{7,6},{8,9},{9,8},{10,11... | collective-permute-start | bytes 884744 | tf_op jit(solution)/shard_map/ppermute | solution.py:307
  19.0 0.0 collective-permute-done.3.rest_2_
  19.0 0.1 collective-permute-start.6
  19.1 5.4 %collective-permute-done.4.rest_3_ = bf16[3,128,384]{2,1,0:T(8,128)(2,1)S(1)} collective-permute-done((bf16[3,128,384]{2,1,0:T(8,128)(2,1)S(1)}, bf16[3,128,384]{2,1,0:T(8,128)(2,1)S(1)}, u32[]{:S(2)}, u32[]{:S(2)}) %collective-permute-start.4) | collective-permute-done | bytes 294944 | tf_op jit(solution)/shard_map/ppermute | solution.py:354
  24.5 5.4 %collective-permute-start.7 = (bf16[3,128,384]{2,1,0:T(8,128)(2,1)S(1)}, bf16[3,128,384]{2,1,0:T(8,128)(2,1)S(1)}, u32[]{:S(2)}, u32[]{:S(2)}) collective-permute-start(bf16[3,128,384]{2,1,0:T(8,128)(2,1)S(1)} %collective-permute-done.4.rest_3_), channel_id=1, source_target_pairs={{0,1},{1,0},{2,3},{3,2},{4,5},{5,4},{6,7},{7,6},{8,9},{9,8},{10,11... | collective-permute-start | bytes 884744 | tf_op jit(solution)/shard_map/ppermute | solution.py:307
  29.9 0.0 collective-permute-done.1.rest_0_
  29.9 0.0 collective-permute-start.8
  29.9 0.0 collective-permute-done.other_w
  29.9 0.0 collective-permute-done.5.rest_4_
  29.9 0.0 collective-permute-done.6.rest_5_
  29.9 1.2 %collective-permute-done.7.rest_6_ = bf16[3,128,384]{2,1,0:T(8,128)(2,1)S(1)} collective-permute-done((bf16[3,128,384]{2,1,0:T(8,128)(2,1)S(1)}, bf16[3,128,384]{2,1,0:T(8,128)(2,1)S(1)}, u32[]{:S(2)}, u32[]{:S(2)}) %collective-permute-start.7) | collective-permute-done | bytes 294944 | tf_op jit(solution)/shard_map/ppermute | solution.py:307
  31.1 0.0 slice-start
  31.1 2.4 %attend_early.1 = (f32[3,512,128]{2,1,0:T(8,128)S(1)}, f32[3,512,128]{2,1,0:T(8,128)S(1)}, f32[3,512,128]{2,1,0:T(8,128)S(1)}) custom-call(f32[512,1024]{1,0:T(8,128)S(1)} %bias.1.bias_ref, bf16[3,128,384]{2,1,0:T(8,128)(2,1)S(1)} %collective-permute-done.1.rest_0_, bf16[3,128,384]{2,1,0:T(8,128)(2,1)S(1)} %collective-permute-done.2.rest_1_, ...), custom_call_target="tpu_custom_call" | custom-call | tf_op jit(solution)/shard_map/attend_early/pallas_call | solution.py:364
  33.6 0.0 collective-permute-done.8.rest_4_
  33.6 0.0 slice-start.1
  33.6 0.6 %attend_late.3 = (bf16[64,384]{1,0:T(8,128)(2,1)S(1)}, bf16[64,384]{1,0:T(8,128)(2,1)S(1)}, bf16[64,384]{1,0:T(8,128)(2,1)S(1)}, bf16[64,384]{1,0:T(8,128)(2,1)S(1)}) custom-call(f32[512,1024]{1,0:T(8,128)S(1)} %bias.1.bias_ref, f32[3,512,128]{2,1,0:T(8,128)S(1)} %get-tuple-element.40.numer_ref, f32[3,512,128]{2,1,0:T(8,128)S(1)} %get-tuple-element.41.total_ref, ...), custom_call_target="tpu_custom_call" | custom-call | tf_op jit(solution)/shard_map/attend_late/pallas_call | solution.py:379
  34.2 3.7 %collective-permute-start.13 = (bf16[64,384]{1,0:T(8,128)(2,1)S(1)}, bf16[64,384]{1,0:T(8,128)(2,1)S(1)}, u32[]{:S(2)}, u32[]{:S(2)}) collective-permute-start(bf16[64,384]{1,0:T(8,128)(2,1)S(1)} %get-tuple-element.49), channel_id=1, source_target_pairs={{0,12},{4,8},{8,4},{12,0},{1,13},{5,9},{9,5},{13,1},{2,14},{6,10},... | collective-permute-start | bytes 147464 | tf_op jit(solution)/shard_map/ppermute | solution.py:396
  38.0 0.6 %collective-permute-start.14 = (bf16[64,384]{1,0:T(8,128)(2,1)S(1)}, bf16[64,384]{1,0:T(8,128)(2,1)S(1)}, u32[]{:S(2)}, u32[]{:S(2)}) collective-permute-start(bf16[64,384]{1,0:T(8,128)(2,1)S(1)} %get-tuple-element.50), channel_id=1, source_target_pairs={{0,8},{4,12},{8,0},{12,4},{1,9},{5,13},{9,1},{13,5},{2,10},{6,14},... | collective-permute-start | bytes 147464 | tf_op jit(solution)/shard_map/ppermute | solution.py:396
  38.6 0.5 collective-permute-start.15
  39.1 0.6 %attend_late.2 = (bf16[64,384]{1,0:T(8,128)(2,1)S(1)}, bf16[64,384]{1,0:T(8,128)(2,1)S(1)}, bf16[64,384]{1,0:T(8,128)(2,1)S(1)}, bf16[64,384]{1,0:T(8,128)(2,1)S(1)}) custom-call(f32[512,1024]{1,0:T(8,128)S(1)} %bias.1.bias_ref, f32[3,512,128]{2,1,0:T(8,128)S(1)} %get-tuple-element.40.numer_ref, f32[3,512,128]{2,1,0:T(8,128)S(1)} %get-tuple-element.41.total_ref, ...), custom_call_target="tpu_custom_call" | custom-call | tf_op jit(solution)/shard_map/attend_late/pallas_call | solution.py:379
  39.7 3.3 %collective-permute-start.9 = (bf16[64,384]{1,0:T(8,128)(2,1)S(1)}, bf16[64,384]{1,0:T(8,128)(2,1)S(1)}, u32[]{:S(2)}, u32[]{:S(2)}) collective-permute-start(bf16[64,384]{1,0:T(8,128)(2,1)S(1)} %get-tuple-element.43), channel_id=1, source_target_pairs={{0,12},{4,8},{8,4},{12,0},{1,13},{5,9},{9,5},{13,1},{2,14},{6,10},... | collective-permute-start | bytes 147464 | tf_op jit(solution)/shard_map/ppermute | solution.py:396
  43.0 0.0 collective-permute-start.10
  43.0 0.0 collective-permute-done.13.rest_0_
  43.0 1.1 %collective-permute-start.11 = (bf16[64,384]{1,0:T(8,128)(2,1)S(1)}, bf16[64,384]{1,0:T(8,128)(2,1)S(1)}, u32[]{:S(2)}, u32[]{:S(2)}) collective-permute-start(bf16[64,384]{1,0:T(8,128)(2,1)S(1)} %get-tuple-element.45), channel_id=1, source_target_pairs={{0,4},{4,0},{8,12},{12,8},{1,5},{5,1},{9,13},{13,9},{2,6},{6,2},{1... | collective-permute-start | bytes 147464 | tf_op jit(solution)/shard_map/ppermute | solution.py:396
  44.2 0.0 collective-permute-done.14.rest_1_
  44.2 0.0 collective-permute-done.15.rest_2_
  44.2 0.0 slice-done
  44.2 0.0 slice-done.1
  44.2 1.8 %project.3 = (f32[32,3072]{1,0:T(8,128)S(1)}, bf16[32,3072]{1,0:T(8,128)(2,1)S(1)}) custom-call(bf16[768,3072]{1,0:T(8,128)(2,1)S(1)} %bitcast.1, bf16[768,3072]{1,0:T(8,128)(2,1)S(1)} %collective-permute-done.other_w, bf16[64,384]{1,0:T(8,128)(2,1)S(1)} %collective-permute-done.13.rest_0_, bf16[64,384]{1,0:T(8,128)(2,1)S(1)} %collective-permute-done.14.rest_1_, ...), custom_call_target="tpu_custom_call" | custom-call | tf_op jit(solution)/shard_map/project/pallas_call | solution.py:402
  46.0 1.6 %collective-permute-start.16 = (bf16[32,3072]{1,0:T(8,128)(2,1)S(1)}, bf16[32,3072]{1,0:T(8,128)(2,1)S(1)}, u32[]{:S(2)}, u32[]{:S(2)}) collective-permute-start(bf16[32,3072]{1,0:T(8,128)(2,1)S(1)} %get-tuple-element.54), channel_id=1, source_target_pairs={{0,2},{2,0},{1,3},{3,1},{4,6},{6,4},{5,7},{7,5},{8,10},{10,8},{9,1... | collective-permute-start | bytes 589832 | tf_op jit(solution)/shard_map/ppermute | solution.py:307
  47.5 0.0 collective-permute-done.9.rest_0_
  47.5 0.8 %collective-permute-done.10.rest_1_ = bf16[64,384]{1,0:T(8,128)(2,1)S(1)} collective-permute-done((bf16[64,384]{1,0:T(8,128)(2,1)S(1)}, bf16[64,384]{1,0:T(8,128)(2,1)S(1)}, u32[]{:S(2)}, u32[]{:S(2)}) %collective-permute-start.10) | collective-permute-done | bytes 49184 | tf_op jit(solution)/shard_map/ppermute | solution.py:396
  48.3 0.0 collective-permute-done.11.rest_2_
  48.3 1.8 %project.2 = (f32[32,3072]{1,0:T(8,128)S(1)}, bf16[32,3072]{1,0:T(8,128)(2,1)S(1)}) custom-call(bf16[768,3072]{1,0:T(8,128)(2,1)S(1)} %bitcast.1, bf16[768,3072]{1,0:T(8,128)(2,1)S(1)} %collective-permute-done.other_w, bf16[64,384]{1,0:T(8,128)(2,1)S(1)} %collective-permute-done.9.rest_0_, bf16[64,384]{1,0:T(8,128)(2,1)S(1)} %collective-permute-done.10.rest_1_, ...), custom_call_target="tpu_custom_call" | custom-call | tf_op jit(solution)/shard_map/project/pallas_call | solution.py:402
  50.1 1.6 %collective-permute-start.12 = (bf16[32,3072]{1,0:T(8,128)(2,1)S(1)}, bf16[32,3072]{1,0:T(8,128)(2,1)S(1)}, u32[]{:S(2)}, u32[]{:S(2)}) collective-permute-start(bf16[32,3072]{1,0:T(8,128)(2,1)S(1)} %get-tuple-element.48), channel_id=1, source_target_pairs={{0,2},{2,0},{1,3},{3,1},{4,6},{6,4},{5,7},{7,5},{8,10},{10,8},{9,1... | collective-permute-start | bytes 589832 | tf_op jit(solution)/shard_map/ppermute | solution.py:307
  51.7 0.8 %collective-permute-done.16.got_ref = bf16[32,3072]{1,0:T(8,128)(2,1)S(1)} collective-permute-done((bf16[32,3072]{1,0:T(8,128)(2,1)S(1)}, bf16[32,3072]{1,0:T(8,128)(2,1)S(1)}, u32[]{:S(2)}, u32[]{:S(2)}) %collective-permute-start.16) | collective-permute-done | bytes 196640 | tf_op jit(solution)/shard_map/ppermute | solution.py:307
  52.5 0.7 %add.2.rest_0_ = bf16[1,64,3072]{2,1,0:T(8,128)(2,1)} custom-call(f32[32,3072]{1,0:T(8,128)S(1)} %get-tuple-element.53.keep_ref, bf16[32,3072]{1,0:T(8,128)(2,1)S(1)} %collective-permute-done.16.got_ref), custom_call_target="tpu_custom_call" | custom-call | tf_op jit(solution)/shard_map/add/pallas_call | solution.py:418
  53.2 2.7 %collective-permute-done.12.got_ref = bf16[32,3072]{1,0:T(8,128)(2,1)S(1)} collective-permute-done((bf16[32,3072]{1,0:T(8,128)(2,1)S(1)}, bf16[32,3072]{1,0:T(8,128)(2,1)S(1)}, u32[]{:S(2)}, u32[]{:S(2)}) %collective-permute-start.12) | collective-permute-done | bytes 196640 | tf_op jit(solution)/shard_map/ppermute | solution.py:307
  55.9 0.7 %add.3 = bf16[1,64,3072]{2,1,0:T(8,128)(2,1)} custom-call(f32[32,3072]{1,0:T(8,128)S(1)} %get-tuple-element.47.keep_ref, bf16[32,3072]{1,0:T(8,128)(2,1)S(1)} %collective-permute-done.12.got_ref, bf16[1,64,3072]{2,1,0:T(8,128)(2,1)} %add.2.rest_0_), custom_call_target="tpu_custom_call", output_to_operand_aliasing={{}: (2, {})} | custom-call | tf_op jit(solution)/shard_map/add/pallas_call | solution.py:418
  (1 shorter events, 0.0 us)
Async XLA Ops:
  1.7 28.2 %collective-permute-start = (bf16[768,3072]{1,0:T(8,128)(2,1)}, bf16[768,3072]{1,0:T(8,128)(2,1)S(1)}, u32[]{:S(2)}, u32[]{:S(2)}) collective-permute-start(bf16[768,3072]{1,0:T(8,128)(2,1)} %own_w.3), channel_id=1, source_target_pairs={{0,1},{1,0},{2,3},{3,2},{4,5},{5,4},{6,7},{7,6},{8,9},{9,8},{10,11... | collective-permute-start | bytes 14155784 | tf_op jit(solution)/shard_map/ppermute | solution.py:307
  2.2 16.8 %collective-permute-start.3 = (bf16[3,128,384]{2,1,0:T(8,128)(2,1)}, bf16[3,128,384]{2,1,0:T(8,128)(2,1)S(1)}, u32[]{:S(2)}, u32[]{:S(2)}) collective-permute-start(bf16[3,128,384]{2,1,0:T(8,128)(2,1)} %pack.2), channel_id=1, source_target_pairs={{0,4},{1,12},{4,5},{5,13},{8,0},{9,8},{12,1},{13,9},{2,6},{3,14},{... | collective-permute-start | bytes 884744 | tf_op jit(solution)/shard_map/ppermute | solution.py:354
  4.9 1.0 %copy-start = (bf16[1,256,768]{2,1,0:T(8,128)(2,1)S(1)}, bf16[1,256,768]{2,1,0:T(8,128)(2,1)}, u32[]{:S(2)}) copy-start(bf16[1,256,768]{2,1,0:T(8,128)(2,1)} %q_ref.2) | copy-start | bytes 1179652
  5.9 1.0 %copy-start.1 = (bf16[1,256,768]{2,1,0:T(8,128)(2,1)S(1)}, bf16[1,256,768]{2,1,0:T(8,128)(2,1)}, u32[]{:S(2)}) copy-start(bf16[1,256,768]{2,1,0:T(8,128)(2,1)} %k_ref.2) | copy-start | bytes 1179652
  6.9 1.0 %copy-start.2 = (bf16[1,256,768]{2,1,0:T(8,128)(2,1)S(1)}, bf16[1,256,768]{2,1,0:T(8,128)(2,1)}, u32[]{:S(2)}) copy-start(bf16[1,256,768]{2,1,0:T(8,128)(2,1)} %v_ref.2) | copy-start | bytes 1179652
  8.1 9.0 %collective-permute-start.2 = (bf16[3,128,384]{2,1,0:T(8,128)(2,1)S(1)}, bf16[3,128,384]{2,1,0:T(8,128)(2,1)S(1)}, u32[]{:S(2)}, u32[]{:S(2)}) collective-permute-start(bf16[3,128,384]{2,1,0:T(8,128)(2,1)S(1)} %get-tuple-element.38), channel_id=1, source_target_pairs={{0,1},{1,9},{4,0},{5,8},{8,5},{9,13},{12,4},{13,12},{2,3},{3,11},{... | collective-permute-start | bytes 884744 | tf_op jit(solution)/shard_map/ppermute | solution.py:354
  10.3 14.1 %collective-permute-start.4 = (bf16[3,128,384]{2,1,0:T(8,128)(2,1)S(1)}, bf16[3,128,384]{2,1,0:T(8,128)(2,1)S(1)}, u32[]{:S(2)}, u32[]{:S(2)}) collective-permute-start(bf16[3,128,384]{2,1,0:T(8,128)(2,1)S(1)} %get-tuple-element.39), channel_id=1, source_target_pairs={{0,5},{1,13},{4,4},{5,12},{8,1},{9,9},{12,0},{13,8},{2,7},{3,15},{... | collective-permute-start | bytes 884744 | tf_op jit(solution)/shard_map/ppermute | solution.py:354
  12.5 0.7 %copy-start.3 = (s32[4,4]{1,0:T(4,128)S(1)}, s32[4,4]{1,0:T(4,128)}, u32[]{:S(2)}) copy-start(s32[4,4]{1,0:T(4,128)} %band_ref.1) | copy-start | bytes 196
  13.1 0.7 %copy-start.4 = (s32[7]{0:T(128)S(1)}, s32[7]{0:T(128)}, u32[]{:S(2)}) copy-start(s32[7]{0:T(128)} %reach_ref.1) | copy-start | bytes 88
  14.5 15.4 %collective-permute-start.1 = (bf16[3,128,384]{2,1,0:T(8,128)(2,1)S(1)}, bf16[3,128,384]{2,1,0:T(8,128)(2,1)S(1)}, u32[]{:S(2)}, u32[]{:S(2)}) collective-permute-start(bf16[3,128,384]{2,1,0:T(8,128)(2,1)S(1)} %get-tuple-element.37), channel_id=1, source_target_pairs={{0,0},{1,8},{4,1},{5,9},{8,4},{9,12},{12,5},{13,13},{2,2},{3,10},{... | collective-permute-start | bytes 884744 | tf_op jit(solution)/shard_map/ppermute | solution.py:354
  17.1 12.8 %collective-permute-start.5 = (bf16[3,128,384]{2,1,0:T(8,128)(2,1)S(1)}, bf16[3,128,384]{2,1,0:T(8,128)(2,1)S(1)}, u32[]{:S(2)}, u32[]{:S(2)}) collective-permute-start(bf16[3,128,384]{2,1,0:T(8,128)(2,1)S(1)} %collective-permute-done.2.rest_1_), channel_id=1, source_target_pairs={{0,1},{1,0},{2,3},{3,2},{4,5},{5,4},{6,7},{7,6},{8,9},{9,8},{10,11... | collective-permute-start | bytes 884744 | tf_op jit(solution)/shard_map/ppermute | solution.py:307
  19.0 11.0 %collective-permute-start.6 = (bf16[3,128,384]{2,1,0:T(8,128)(2,1)S(1)}, bf16[3,128,384]{2,1,0:T(8,128)(2,1)S(1)}, u32[]{:S(2)}, u32[]{:S(2)}) collective-permute-start(bf16[3,128,384]{2,1,0:T(8,128)(2,1)S(1)} %collective-permute-done.3.rest_2_), channel_id=1, source_target_pairs={{0,1},{1,0},{2,3},{3,2},{4,5},{5,4},{6,7},{7,6},{8,9},{9,8},{10,11... | collective-permute-start | bytes 884744 | tf_op jit(solution)/shard_map/ppermute | solution.py:307
  24.5 6.7 %collective-permute-start.7 = (bf16[3,128,384]{2,1,0:T(8,128)(2,1)S(1)}, bf16[3,128,384]{2,1,0:T(8,128)(2,1)S(1)}, u32[]{:S(2)}, u32[]{:S(2)}) collective-permute-start(bf16[3,128,384]{2,1,0:T(8,128)(2,1)S(1)} %collective-permute-done.4.rest_3_), channel_id=1, source_target_pairs={{0,1},{1,0},{2,3},{3,2},{4,5},{5,4},{6,7},{7,6},{8,9},{9,8},{10,11... | collective-permute-start | bytes 884744 | tf_op jit(solution)/shard_map/ppermute | solution.py:307
  29.9 3.7 %collective-permute-start.8 = (bf16[3,128,384]{2,1,0:T(8,128)(2,1)S(1)}, bf16[3,128,384]{2,1,0:T(8,128)(2,1)S(1)}, u32[]{:S(2)}, u32[]{:S(2)}) collective-permute-start(bf16[3,128,384]{2,1,0:T(8,128)(2,1)S(1)} %collective-permute-done.1.rest_0_), channel_id=1, source_target_pairs={{0,1},{1,0},{2,3},{3,2},{4,5},{5,4},{6,7},{7,6},{8,9},{9,8},{10,11... | collective-permute-start | bytes 884744 | tf_op jit(solution)/shard_map/ppermute | solution.py:307
  31.1 13.0 %slice-start = ((s8[4718592]{0:T(1024)(128)(4,1)}), s8[4194304]{0:T(1024)(128)(4,1)S(1)}, s32[]{:S(2)}) async-start(s8[4718592]{0:T(1024)(128)(4,1)} %bitcast), calls=%async_computation | async-start | bytes 8388608
  33.6 10.6 %slice-start.1 = ((s8[4718592]{0:T(1024)(128)(4,1)}), s8[524288]{0:T(1024)(128)(4,1)S(1)}, s32[]{:S(2)}) async-start(s8[4718592]{0:T(1024)(128)(4,1)} %bitcast), calls=%async_computation.1 | async-start | bytes 1048576
  34.2 8.8 %collective-permute-start.13 = (bf16[64,384]{1,0:T(8,128)(2,1)S(1)}, bf16[64,384]{1,0:T(8,128)(2,1)S(1)}, u32[]{:S(2)}, u32[]{:S(2)}) collective-permute-start(bf16[64,384]{1,0:T(8,128)(2,1)S(1)} %get-tuple-element.49), channel_id=1, source_target_pairs={{0,12},{4,8},{8,4},{12,0},{1,13},{5,9},{9,5},{13,1},{2,14},{6,10},... | collective-permute-start | bytes 147464 | tf_op jit(solution)/shard_map/ppermute | solution.py:396
  38.0 6.2 %collective-permute-start.14 = (bf16[64,384]{1,0:T(8,128)(2,1)S(1)}, bf16[64,384]{1,0:T(8,128)(2,1)S(1)}, u32[]{:S(2)}, u32[]{:S(2)}) collective-permute-start(bf16[64,384]{1,0:T(8,128)(2,1)S(1)} %get-tuple-element.50), channel_id=1, source_target_pairs={{0,8},{4,12},{8,0},{12,4},{1,9},{5,13},{9,1},{13,5},{2,10},{6,14},... | collective-permute-start | bytes 147464 | tf_op jit(solution)/shard_map/ppermute | solution.py:396
  38.6 5.6 %collective-permute-start.15 = (bf16[64,384]{1,0:T(8,128)(2,1)S(1)}, bf16[64,384]{1,0:T(8,128)(2,1)S(1)}, u32[]{:S(2)}, u32[]{:S(2)}) collective-permute-start(bf16[64,384]{1,0:T(8,128)(2,1)S(1)} %get-tuple-element.51), channel_id=1, source_target_pairs={{0,4},{4,0},{8,12},{12,8},{1,5},{5,1},{9,13},{13,9},{2,6},{6,2},{1... | collective-permute-start | bytes 147464 | tf_op jit(solution)/shard_map/ppermute | solution.py:396
  39.7 7.8 %collective-permute-start.9 = (bf16[64,384]{1,0:T(8,128)(2,1)S(1)}, bf16[64,384]{1,0:T(8,128)(2,1)S(1)}, u32[]{:S(2)}, u32[]{:S(2)}) collective-permute-start(bf16[64,384]{1,0:T(8,128)(2,1)S(1)} %get-tuple-element.43), channel_id=1, source_target_pairs={{0,12},{4,8},{8,4},{12,0},{1,13},{5,9},{9,5},{13,1},{2,14},{6,10},... | collective-permute-start | bytes 147464 | tf_op jit(solution)/shard_map/ppermute | solution.py:396
  43.0 5.3 %collective-permute-start.10 = (bf16[64,384]{1,0:T(8,128)(2,1)S(1)}, bf16[64,384]{1,0:T(8,128)(2,1)S(1)}, u32[]{:S(2)}, u32[]{:S(2)}) collective-permute-start(bf16[64,384]{1,0:T(8,128)(2,1)S(1)} %get-tuple-element.44), channel_id=1, source_target_pairs={{0,8},{4,12},{8,0},{12,4},{1,9},{5,13},{9,1},{13,5},{2,10},{6,14},... | collective-permute-start | bytes 147464 | tf_op jit(solution)/shard_map/ppermute | solution.py:396
  43.0 5.3 %collective-permute-start.11 = (bf16[64,384]{1,0:T(8,128)(2,1)S(1)}, bf16[64,384]{1,0:T(8,128)(2,1)S(1)}, u32[]{:S(2)}, u32[]{:S(2)}) collective-permute-start(bf16[64,384]{1,0:T(8,128)(2,1)S(1)} %get-tuple-element.45), channel_id=1, source_target_pairs={{0,4},{4,0},{8,12},{12,8},{1,5},{5,1},{9,13},{13,9},{2,6},{6,2},{1... | collective-permute-start | bytes 147464 | tf_op jit(solution)/shard_map/ppermute | solution.py:396
  46.0 6.5 %collective-permute-start.16 = (bf16[32,3072]{1,0:T(8,128)(2,1)S(1)}, bf16[32,3072]{1,0:T(8,128)(2,1)S(1)}, u32[]{:S(2)}, u32[]{:S(2)}) collective-permute-start(bf16[32,3072]{1,0:T(8,128)(2,1)S(1)} %get-tuple-element.54), channel_id=1, source_target_pairs={{0,2},{2,0},{1,3},{3,1},{4,6},{6,4},{5,7},{7,5},{8,10},{10,8},{9,1... | collective-permute-start | bytes 589832 | tf_op jit(solution)/shard_map/ppermute | solution.py:307
  50.1 5.8 %collective-permute-start.12 = (bf16[32,3072]{1,0:T(8,128)(2,1)S(1)}, bf16[32,3072]{1,0:T(8,128)(2,1)S(1)}, u32[]{:S(2)}, u32[]{:S(2)}) collective-permute-start(bf16[32,3072]{1,0:T(8,128)(2,1)S(1)} %get-tuple-element.48), channel_id=1, source_target_pairs={{0,2},{2,0},{1,3},{3,1},{4,6},{6,4},{5,7},{7,5},{8,10},{10,8},{9,1... | collective-permute-start | bytes 589832 | tf_op jit(solution)/shard_map/ppermute | solution.py:307

commit v2 on v1

--- a/solution.py
+++ b/solution.py
@@ -331,7 +331,7 @@
     packed = dict(zip(FIRST, pack(FIRST, PACK_MB, queries, keys, values)))
     others = [r for r in range(n) if r not in FIRST]
     arrays = lax.optimization_barrier((queries, keys, values, packed[FIRST[0]]))[:3]
-    packed.update(zip(others, pack(others, 6, *arrays)))
+    packed.update(zip(others, pack(others, PACK_MB, *arrays)))
     per = n // cores
     rounds = [
         [

time: 57 us -> 56.9 us (level)
  local copies, waits for them, and re-layouts: 4.33 us -> 1.34 us
  Pallas kernels: 11.4 us -> 13.4 us
  starting transfers between devices: 28 us -> 28.6 us
    unnamed x14 -> x8, local copies, waits for them, and re-layouts: 4.33 us -> 1.34 us
    pallas_call x2, Pallas kernels: 1.94 us -> 3.92 us  [pack(): pl.pallas_call(functools.partial(pack_kernel, n, cores, tokens, rounds),...]
    ppermute x4, starting transfers between devices: 7.65 us -> 8.6 us  [spread(): own = [lax.ppermute(blocks[r], ('tm', 'sub'), rounds[r]) for r in range(n)]]
  transfers between devices with their start and end apart: 17 -> 17, of which waited for: 6 -> 6; matrix products, arithmetic and copies ran while one was open for 0% -> 0% of each run, Pallas kernels for 15% -> 18%
where the time goes in v2:
time: 56.9 us; the launch traced here: 56.7 us
  starting transfers between devices  28.6 us (50%)
  Pallas kernels  13.4 us (24%)
  waiting for transfers between devices  13.2 us (23%)
  local copies, waits for them, and re-layouts  1.34 us (2%)
    ppermute x7, starting transfers between devices, swapped(): return lax.ppermute(x, axis, [(0, 1), (1, 0)])  10.5 us
    ppermute x6, starting transfers between devices, spread(): back.append((k, [a], lax.ppermute(out, 'tm', pairs) if k else out))  9.53 us
    ppermute x4, starting transfers between devices, spread(): own = [lax.ppermute(blocks[r], ('tm', 'sub'), rounds[r]) for r in range(n)]  8.6 us
    ppermute x4, waiting for transfers between devices, spread(): own = [lax.ppermute(blocks[r], ('tm', 'sub'), rounds[r]) for r in range(n)]  7.66 us
    ppermute x7, waiting for transfers between devices, swapped(): return lax.ppermute(x, axis, [(0, 1), (1, 0)])  4.71 us
    pallas_call x2, Pallas kernels, pack(): pl.pallas_call(functools.partial(pack_kernel, n, cores, tokens, rounds),...  3.92 us
    pallas_call x2, Pallas kernels, spread(): pl.pallas_call(functools.partial(project_kernel, n, cores, places), out_s...  3.59 us
    pallas_call x1, Pallas kernels, spread(): pl.pallas_call(functools.partial(attend_early_kernel, n, cores, tokens),...  2.44 us
  transfers between devices with their start and end apart: 17, of which 6 were waited for; matrix products, arithmetic and copies ran while one was open for 0% of the time, Pallas kernels for 18%

profile of v2, /device:TPU:0, one launch (start us, length us, event | category | flops | bytes accessed | tf_op | source)
XLA Modules:
  0.0 56.7 jit_solution(18226559123199256232)
XLA Ops:
  0.0 1.7 %pack.2 = bf16[3,128,384]{2,1,0:T(8,128)(2,1)} custom-call(bf16[1,256,768]{2,1,0:T(8,128)(2,1)} %q_ref.2, bf16[1,256,768]{2,1,0:T(8,128)(2,1)} %k_ref.2, bf16[1,256,768]{2,1,0:T(8,128)(2,1)} %v_ref.2), custom_call_target="tpu_custom_call" | custom-call | tf_op jit(solution)/shard_map/pack/pallas_call | solution.py:321
  1.7 0.5 collective-permute-start
  2.2 2.6 %collective-permute-start.3 = (bf16[3,128,384]{2,1,0:T(8,128)(2,1)}, bf16[3,128,384]{2,1,0:T(8,128)(2,1)S(1)}, u32[]{:S(2)}, u32[]{:S(2)}) collective-permute-start(bf16[3,128,384]{2,1,0:T(8,128)(2,1)} %pack.2), channel_id=1, source_target_pairs={{0,4},{1,12},{4,5},{5,13},{8,0},{9,8},{12,1},{13,9},{2,6},{3,14},{... | collective-permute-start | bytes 884744 | tf_op jit(solution)/shard_map/ppermute | solution.py:354
  4.9 2.2 %pack.3 = (bf16[3,128,384]{2,1,0:T(8,128)(2,1)}, bf16[3,128,384]{2,1,0:T(8,128)(2,1)}, bf16[3,128,384]{2,1,0:T(8,128)(2,1)}) custom-call(bf16[1,256,768]{2,1,0:T(8,128)(2,1)} %q_ref.2, bf16[1,256,768]{2,1,0:T(8,128)(2,1)} %k_ref.2, bf16[1,256,768]{2,1,0:T(8,128)(2,1)} %v_ref.2), custom_call_target="tpu_custom_call" | custom-call | tf_op jit(solution)/shard_map/pack/pallas_call | solution.py:321
  7.1 2.2 %collective-permute-start.2 = (bf16[3,128,384]{2,1,0:T(8,128)(2,1)}, bf16[3,128,384]{2,1,0:T(8,128)(2,1)S(1)}, u32[]{:S(2)}, u32[]{:S(2)}) collective-permute-start(bf16[3,128,384]{2,1,0:T(8,128)(2,1)} %get-tuple-element.38), channel_id=1, source_target_pairs={{0,1},{1,9},{4,0},{5,8},{8,5},{9,13},{12,4},{13,12},{2,3},{3,11},{... | collective-permute-start | bytes 884744 | tf_op jit(solution)/shard_map/ppermute | solution.py:354
  9.3 2.1 %collective-permute-start.4 = (bf16[3,128,384]{2,1,0:T(8,128)(2,1)}, bf16[3,128,384]{2,1,0:T(8,128)(2,1)S(1)}, u32[]{:S(2)}, u32[]{:S(2)}) collective-permute-start(bf16[3,128,384]{2,1,0:T(8,128)(2,1)} %get-tuple-element.39), channel_id=1, source_target_pairs={{0,5},{1,13},{4,4},{5,12},{8,1},{9,9},{12,0},{13,8},{2,7},{3,15},{... | collective-permute-start | bytes 884744 | tf_op jit(solution)/shard_map/ppermute | solution.py:354
  11.4 0.0 copy-start
  11.4 0.7 %copy-done = s32[4,4]{1,0:T(4,128)S(1)} copy-done((s32[4,4]{1,0:T(4,128)S(1)}, s32[4,4]{1,0:T(4,128)}, u32[]{:S(2)}) %copy-start) | copy-done | bytes 88
  12.1 0.0 copy-start.1
  12.1 0.7 %copy-done.1 = s32[7]{0:T(128)S(1)} copy-done((s32[7]{0:T(128)S(1)}, s32[7]{0:T(128)}, u32[]{:S(2)}) %copy-start.1) | copy-done | bytes 52
  12.8 0.7 %bias.1.bias_ref = f32[512,1024]{1,0:T(8,128)S(1)} custom-call(s32[4,4]{1,0:T(4,128)S(1)} %copy-done, s32[7]{0:T(128)S(1)} %copy-done.1), custom_call_target="tpu_custom_call" | custom-call | tf_op jit(solution)/shard_map/bias/pallas_call | solution.py:344
  13.5 1.6 %collective-permute-start.1 = (bf16[3,128,384]{2,1,0:T(8,128)(2,1)}, bf16[3,128,384]{2,1,0:T(8,128)(2,1)S(1)}, u32[]{:S(2)}, u32[]{:S(2)}) collective-permute-start(bf16[3,128,384]{2,1,0:T(8,128)(2,1)} %get-tuple-element.37), channel_id=1, source_target_pairs={{0,0},{1,8},{4,1},{5,9},{8,4},{9,12},{12,5},{13,13},{2,2},{3,10},{... | collective-permute-start | bytes 884744 | tf_op jit(solution)/shard_map/ppermute | solution.py:354
  15.1 2.0 %collective-permute-done.2.rest_1_ = bf16[3,128,384]{2,1,0:T(8,128)(2,1)S(1)} collective-permute-done((bf16[3,128,384]{2,1,0:T(8,128)(2,1)}, bf16[3,128,384]{2,1,0:T(8,128)(2,1)S(1)}, u32[]{:S(2)}, u32[]{:S(2)}) %collective-permute-start.2) | collective-permute-done | bytes 294944 | tf_op jit(solution)/shard_map/ppermute | solution.py:354
  17.1 1.6 %collective-permute-start.5 = (bf16[3,128,384]{2,1,0:T(8,128)(2,1)S(1)}, bf16[3,128,384]{2,1,0:T(8,128)(2,1)S(1)}, u32[]{:S(2)}, u32[]{:S(2)}) collective-permute-start(bf16[3,128,384]{2,1,0:T(8,128)(2,1)S(1)} %collective-permute-done.2.rest_1_), channel_id=1, source_target_pairs={{0,1},{1,0},{2,3},{3,2},{4,5},{5,4},{6,7},{7,6},{8,9},{9,8},{10,11... | collective-permute-start | bytes 884744 | tf_op jit(solution)/shard_map/ppermute | solution.py:307
  18.7 0.0 collective-permute-done.3.rest_2_
  18.7 0.0 collective-permute-start.6
  18.7 5.7 %collective-permute-done.4.rest_3_ = bf16[3,128,384]{2,1,0:T(8,128)(2,1)S(1)} collective-permute-done((bf16[3,128,384]{2,1,0:T(8,128)(2,1)}, bf16[3,128,384]{2,1,0:T(8,128)(2,1)S(1)}, u32[]{:S(2)}, u32[]{:S(2)}) %collective-permute-start.4) | collective-permute-done | bytes 294944 | tf_op jit(solution)/shard_map/ppermute | solution.py:354
  24.4 5.2 %collective-permute-start.7 = (bf16[3,128,384]{2,1,0:T(8,128)(2,1)S(1)}, bf16[3,128,384]{2,1,0:T(8,128)(2,1)S(1)}, u32[]{:S(2)}, u32[]{:S(2)}) collective-permute-start(bf16[3,128,384]{2,1,0:T(8,128)(2,1)S(1)} %collective-permute-done.4.rest_3_), channel_id=1, source_target_pairs={{0,1},{1,0},{2,3},{3,2},{4,5},{5,4},{6,7},{7,6},{8,9},{9,8},{10,11... | collective-permute-start | bytes 884744 | tf_op jit(solution)/shard_map/ppermute | solution.py:307
  29.7 0.0 collective-permute-done.1.rest_0_
  29.7 0.0 collective-permute-start.8
  29.7 0.0 collective-permute-done.other_w
  29.7 0.0 collective-permute-done.5.rest_4_
  29.7 0.0 collective-permute-done.6.rest_5_
  29.7 1.2 %collective-permute-done.7.rest_6_ = bf16[3,128,384]{2,1,0:T(8,128)(2,1)S(1)} collective-permute-done((bf16[3,128,384]{2,1,0:T(8,128)(2,1)S(1)}, bf16[3,128,384]{2,1,0:T(8,128)(2,1)S(1)}, u32[]{:S(2)}, u32[]{:S(2)}) %collective-permute-start.7) | collective-permute-done | bytes 294944 | tf_op jit(solution)/shard_map/ppermute | solution.py:307
  30.9 0.0 slice-start
  30.9 2.4 %attend_early.1 = (f32[3,512,128]{2,1,0:T(8,128)S(1)}, f32[3,512,128]{2,1,0:T(8,128)S(1)}, f32[3,512,128]{2,1,0:T(8,128)S(1)}) custom-call(f32[512,1024]{1,0:T(8,128)S(1)} %bias.1.bias_ref, bf16[3,128,384]{2,1,0:T(8,128)(2,1)S(1)} %collective-permute-done.1.rest_0_, bf16[3,128,384]{2,1,0:T(8,128)(2,1)S(1)} %collective-permute-done.2.rest_1_, ...), custom_call_target="tpu_custom_call" | custom-call | tf_op jit(solution)/shard_map/attend_early/pallas_call | solution.py:364
  33.3 0.0 collective-permute-done.8.rest_4_
  33.3 0.0 slice-start.1
  33.3 0.6 %attend_late.3 = (bf16[64,384]{1,0:T(8,128)(2,1)S(1)}, bf16[64,384]{1,0:T(8,128)(2,1)S(1)}, bf16[64,384]{1,0:T(8,128)(2,1)S(1)}, bf16[64,384]{1,0:T(8,128)(2,1)S(1)}) custom-call(f32[512,1024]{1,0:T(8,128)S(1)} %bias.1.bias_ref, f32[3,512,128]{2,1,0:T(8,128)S(1)} %get-tuple-element.40.numer_ref, f32[3,512,128]{2,1,0:T(8,128)S(1)} %get-tuple-element.41.total_ref, ...), custom_call_target="tpu_custom_call" | custom-call | tf_op jit(solution)/shard_map/attend_late/pallas_call | solution.py:379
  34.0 4.0 %collective-permute-start.13 = (bf16[64,384]{1,0:T(8,128)(2,1)S(1)}, bf16[64,384]{1,0:T(8,128)(2,1)S(1)}, u32[]{:S(2)}, u32[]{:S(2)}) collective-permute-start(bf16[64,384]{1,0:T(8,128)(2,1)S(1)} %get-tuple-element.49), channel_id=1, source_target_pairs={{0,12},{4,8},{8,4},{12,0},{1,13},{5,9},{9,5},{13,1},{2,14},{6,10},... | collective-permute-start | bytes 147464 | tf_op jit(solution)/shard_map/ppermute | solution.py:396
  38.0 0.6 %collective-permute-start.14 = (bf16[64,384]{1,0:T(8,128)(2,1)S(1)}, bf16[64,384]{1,0:T(8,128)(2,1)S(1)}, u32[]{:S(2)}, u32[]{:S(2)}) collective-permute-start(bf16[64,384]{1,0:T(8,128)(2,1)S(1)} %get-tuple-element.50), channel_id=1, source_target_pairs={{0,8},{4,12},{8,0},{12,4},{1,9},{5,13},{9,1},{13,5},{2,10},{6,14},... | collective-permute-start | bytes 147464 | tf_op jit(solution)/shard_map/ppermute | solution.py:396
  38.6 0.5 collective-permute-start.15
  39.1 0.6 %attend_late.2 = (bf16[64,384]{1,0:T(8,128)(2,1)S(1)}, bf16[64,384]{1,0:T(8,128)(2,1)S(1)}, bf16[64,384]{1,0:T(8,128)(2,1)S(1)}, bf16[64,384]{1,0:T(8,128)(2,1)S(1)}) custom-call(f32[512,1024]{1,0:T(8,128)S(1)} %bias.1.bias_ref, f32[3,512,128]{2,1,0:T(8,128)S(1)} %get-tuple-element.40.numer_ref, f32[3,512,128]{2,1,0:T(8,128)S(1)} %get-tuple-element.41.total_ref, ...), custom_call_target="tpu_custom_call" | custom-call | tf_op jit(solution)/shard_map/attend_late/pallas_call | solution.py:379
  39.7 3.3 %collective-permute-start.9 = (bf16[64,384]{1,0:T(8,128)(2,1)S(1)}, bf16[64,384]{1,0:T(8,128)(2,1)S(1)}, u32[]{:S(2)}, u32[]{:S(2)}) collective-permute-start(bf16[64,384]{1,0:T(8,128)(2,1)S(1)} %get-tuple-element.43), channel_id=1, source_target_pairs={{0,12},{4,8},{8,4},{12,0},{1,13},{5,9},{9,5},{13,1},{2,14},{6,10},... | collective-permute-start | bytes 147464 | tf_op jit(solution)/shard_map/ppermute | solution.py:396
  43.0 0.0 collective-permute-start.10
  43.1 0.0 collective-permute-done.13.rest_0_
  43.1 1.1 %collective-permute-start.11 = (bf16[64,384]{1,0:T(8,128)(2,1)S(1)}, bf16[64,384]{1,0:T(8,128)(2,1)S(1)}, u32[]{:S(2)}, u32[]{:S(2)}) collective-permute-start(bf16[64,384]{1,0:T(8,128)(2,1)S(1)} %get-tuple-element.45), channel_id=1, source_target_pairs={{0,4},{4,0},{8,12},{12,8},{1,5},{5,1},{9,13},{13,9},{2,6},{6,2},{1... | collective-permute-start | bytes 147464 | tf_op jit(solution)/shard_map/ppermute | solution.py:396
  44.2 0.0 collective-permute-done.14.rest_1_
  44.2 0.0 collective-permute-done.15.rest_2_
  44.2 0.0 slice-done
  44.2 0.0 slice-done.1
  44.2 1.8 %project.3 = (f32[32,3072]{1,0:T(8,128)S(1)}, bf16[32,3072]{1,0:T(8,128)(2,1)S(1)}) custom-call(bf16[768,3072]{1,0:T(8,128)(2,1)S(1)} %bitcast.1, bf16[768,3072]{1,0:T(8,128)(2,1)S(1)} %collective-permute-done.other_w, bf16[64,384]{1,0:T(8,128)(2,1)S(1)} %collective-permute-done.13.rest_0_, bf16[64,384]{1,0:T(8,128)(2,1)S(1)} %collective-permute-done.14.rest_1_, ...), custom_call_target="tpu_custom_call" | custom-call | tf_op jit(solution)/shard_map/project/pallas_call | solution.py:402
  46.0 1.5 %collective-permute-start.16 = (bf16[32,3072]{1,0:T(8,128)(2,1)S(1)}, bf16[32,3072]{1,0:T(8,128)(2,1)S(1)}, u32[]{:S(2)}, u32[]{:S(2)}) collective-permute-start(bf16[32,3072]{1,0:T(8,128)(2,1)S(1)} %get-tuple-element.54), channel_id=1, source_target_pairs={{0,2},{2,0},{1,3},{3,1},{4,6},{6,4},{5,7},{7,5},{8,10},{10,8},{9,1... | collective-permute-start | bytes 589832 | tf_op jit(solution)/shard_map/ppermute | solution.py:307
  47.5 0.0 collective-permute-done.9.rest_0_
  47.5 0.8 %collective-permute-done.10.rest_1_ = bf16[64,384]{1,0:T(8,128)(2,1)S(1)} collective-permute-done((bf16[64,384]{1,0:T(8,128)(2,1)S(1)}, bf16[64,384]{1,0:T(8,128)(2,1)S(1)}, u32[]{:S(2)}, u32[]{:S(2)}) %collective-permute-start.10) | collective-permute-done | bytes 49184 | tf_op jit(solution)/shard_map/ppermute | solution.py:396
  48.3 0.0 collective-permute-done.11.rest_2_
  48.3 1.8 %project.2 = (f32[32,3072]{1,0:T(8,128)S(1)}, bf16[32,3072]{1,0:T(8,128)(2,1)S(1)}) custom-call(bf16[768,3072]{1,0:T(8,128)(2,1)S(1)} %bitcast.1, bf16[768,3072]{1,0:T(8,128)(2,1)S(1)} %collective-permute-done.other_w, bf16[64,384]{1,0:T(8,128)(2,1)S(1)} %collective-permute-done.9.rest_0_, bf16[64,384]{1,0:T(8,128)(2,1)S(1)} %collective-permute-done.10.rest_1_, ...), custom_call_target="tpu_custom_call" | custom-call | tf_op jit(solution)/shard_map/project/pallas_call | solution.py:402
  50.1 1.5 %collective-permute-start.12 = (bf16[32,3072]{1,0:T(8,128)(2,1)S(1)}, bf16[32,3072]{1,0:T(8,128)(2,1)S(1)}, u32[]{:S(2)}, u32[]{:S(2)}) collective-permute-start(bf16[32,3072]{1,0:T(8,128)(2,1)S(1)} %get-tuple-element.48), channel_id=1, source_target_pairs={{0,2},{2,0},{1,3},{3,1},{4,6},{6,4},{5,7},{7,5},{8,10},{10,8},{9,1... | collective-permute-start | bytes 589832 | tf_op jit(solution)/shard_map/ppermute | solution.py:307
  51.7 0.8 %collective-permute-done.16.got_ref = bf16[32,3072]{1,0:T(8,128)(2,1)S(1)} collective-permute-done((bf16[32,3072]{1,0:T(8,128)(2,1)S(1)}, bf16[32,3072]{1,0:T(8,128)(2,1)S(1)}, u32[]{:S(2)}, u32[]{:S(2)}) %collective-permute-start.16) | collective-permute-done | bytes 196640 | tf_op jit(solution)/shard_map/ppermute | solution.py:307
  52.5 0.7 %add.2.rest_0_ = bf16[1,64,3072]{2,1,0:T(8,128)(2,1)} custom-call(f32[32,3072]{1,0:T(8,128)S(1)} %get-tuple-element.53.keep_ref, bf16[32,3072]{1,0:T(8,128)(2,1)S(1)} %collective-permute-done.16.got_ref), custom_call_target="tpu_custom_call" | custom-call | tf_op jit(solution)/shard_map/add/pallas_call | solution.py:418
  53.2 2.7 %collective-permute-done.12.got_ref = bf16[32,3072]{1,0:T(8,128)(2,1)S(1)} collective-permute-done((bf16[32,3072]{1,0:T(8,128)(2,1)S(1)}, bf16[32,3072]{1,0:T(8,128)(2,1)S(1)}, u32[]{:S(2)}, u32[]{:S(2)}) %collective-permute-start.12) | collective-permute-done | bytes 196640 | tf_op jit(solution)/shard_map/ppermute | solution.py:307
  55.9 0.7 %add.3 = bf16[1,64,3072]{2,1,0:T(8,128)(2,1)} custom-call(f32[32,3072]{1,0:T(8,128)S(1)} %get-tuple-element.47.keep_ref, bf16[32,3072]{1,0:T(8,128)(2,1)S(1)} %collective-permute-done.12.got_ref, bf16[1,64,3072]{2,1,0:T(8,128)(2,1)} %add.2.rest_0_), custom_call_target="tpu_custom_call", output_to_operand_aliasing={{}: (2, {})} | custom-call | tf_op jit(solution)/shard_map/add/pallas_call | solution.py:418
  (1 shorter events, 0.0 us)
Async XLA Ops:
  1.7 28.0 %collective-permute-start = (bf16[768,3072]{1,0:T(8,128)(2,1)}, bf16[768,3072]{1,0:T(8,128)(2,1)S(1)}, u32[]{:S(2)}, u32[]{:S(2)}) collective-permute-start(bf16[768,3072]{1,0:T(8,128)(2,1)} %own_w.3), channel_id=1, source_target_pairs={{0,1},{1,0},{2,3},{3,2},{4,5},{5,4},{6,7},{7,6},{8,9},{9,8},{10,11... | collective-permute-start | bytes 14155784 | tf_op jit(solution)/shard_map/ppermute | solution.py:307
  2.2 16.5 %collective-permute-start.3 = (bf16[3,128,384]{2,1,0:T(8,128)(2,1)}, bf16[3,128,384]{2,1,0:T(8,128)(2,1)S(1)}, u32[]{:S(2)}, u32[]{:S(2)}) collective-permute-start(bf16[3,128,384]{2,1,0:T(8,128)(2,1)} %pack.2), channel_id=1, source_target_pairs={{0,4},{1,12},{4,5},{5,13},{8,0},{9,8},{12,1},{13,9},{2,6},{3,14},{... | collective-permute-start | bytes 884744 | tf_op jit(solution)/shard_map/ppermute | solution.py:354
  7.1 10.0 %collective-permute-start.2 = (bf16[3,128,384]{2,1,0:T(8,128)(2,1)}, bf16[3,128,384]{2,1,0:T(8,128)(2,1)S(1)}, u32[]{:S(2)}, u32[]{:S(2)}) collective-permute-start(bf16[3,128,384]{2,1,0:T(8,128)(2,1)} %get-tuple-element.38), channel_id=1, source_target_pairs={{0,1},{1,9},{4,0},{5,8},{8,5},{9,13},{12,4},{13,12},{2,3},{3,11},{... | collective-permute-start | bytes 884744 | tf_op jit(solution)/shard_map/ppermute | solution.py:354
  9.3 15.1 %collective-permute-start.4 = (bf16[3,128,384]{2,1,0:T(8,128)(2,1)}, bf16[3,128,384]{2,1,0:T(8,128)(2,1)S(1)}, u32[]{:S(2)}, u32[]{:S(2)}) collective-permute-start(bf16[3,128,384]{2,1,0:T(8,128)(2,1)} %get-tuple-element.39), channel_id=1, source_target_pairs={{0,5},{1,13},{4,4},{5,12},{8,1},{9,9},{12,0},{13,8},{2,7},{3,15},{... | collective-permute-start | bytes 884744 | tf_op jit(solution)/shard_map/ppermute | solution.py:354
  11.4 0.7 %copy-start = (s32[4,4]{1,0:T(4,128)S(1)}, s32[4,4]{1,0:T(4,128)}, u32[]{:S(2)}) copy-start(s32[4,4]{1,0:T(4,128)} %band_ref.1) | copy-start | bytes 196
  12.1 0.7 %copy-start.1 = (s32[7]{0:T(128)S(1)}, s32[7]{0:T(128)}, u32[]{:S(2)}) copy-start(s32[7]{0:T(128)} %reach_ref.1) | copy-start | bytes 88
  13.5 16.1 %collective-permute-start.1 = (bf16[3,128,384]{2,1,0:T(8,128)(2,1)}, bf16[3,128,384]{2,1,0:T(8,128)(2,1)S(1)}, u32[]{:S(2)}, u32[]{:S(2)}) collective-permute-start(bf16[3,128,384]{2,1,0:T(8,128)(2,1)} %get-tuple-element.37), channel_id=1, source_target_pairs={{0,0},{1,8},{4,1},{5,9},{8,4},{9,12},{12,5},{13,13},{2,2},{3,10},{... | collective-permute-start | bytes 884744 | tf_op jit(solution)/shard_map/ppermute | solution.py:354
  17.1 12.6 %collective-permute-start.5 = (bf16[3,128,384]{2,1,0:T(8,128)(2,1)S(1)}, bf16[3,128,384]{2,1,0:T(8,128)(2,1)S(1)}, u32[]{:S(2)}, u32[]{:S(2)}) collective-permute-start(bf16[3,128,384]{2,1,0:T(8,128)(2,1)S(1)} %collective-permute-done.2.rest_1_), channel_id=1, source_target_pairs={{0,1},{1,0},{2,3},{3,2},{4,5},{5,4},{6,7},{7,6},{8,9},{9,8},{10,11... | collective-permute-start | bytes 884744 | tf_op jit(solution)/shard_map/ppermute | solution.py:307
  18.7 10.9 %collective-permute-start.6 = (bf16[3,128,384]{2,1,0:T(8,128)(2,1)S(1)}, bf16[3,128,384]{2,1,0:T(8,128)(2,1)S(1)}, u32[]{:S(2)}, u32[]{:S(2)}) collective-permute-start(bf16[3,128,384]{2,1,0:T(8,128)(2,1)S(1)} %collective-permute-done.3.rest_2_), channel_id=1, source_target_pairs={{0,1},{1,0},{2,3},{3,2},{4,5},{5,4},{6,7},{7,6},{8,9},{9,8},{10,11... | collective-permute-start | bytes 884744 | tf_op jit(solution)/shard_map/ppermute | solution.py:307
  24.4 6.4 %collective-permute-start.7 = (bf16[3,128,384]{2,1,0:T(8,128)(2,1)S(1)}, bf16[3,128,384]{2,1,0:T(8,128)(2,1)S(1)}, u32[]{:S(2)}, u32[]{:S(2)}) collective-permute-start(bf16[3,128,384]{2,1,0:T(8,128)(2,1)S(1)} %collective-permute-done.4.rest_3_), channel_id=1, source_target_pairs={{0,1},{1,0},{2,3},{3,2},{4,5},{5,4},{6,7},{7,6},{8,9},{9,8},{10,11... | collective-permute-start | bytes 884744 | tf_op jit(solution)/shard_map/ppermute | solution.py:307
  29.7 3.7 %collective-permute-start.8 = (bf16[3,128,384]{2,1,0:T(8,128)(2,1)S(1)}, bf16[3,128,384]{2,1,0:T(8,128)(2,1)S(1)}, u32[]{:S(2)}, u32[]{:S(2)}) collective-permute-start(bf16[3,128,384]{2,1,0:T(8,128)(2,1)S(1)} %collective-permute-done.1.rest_0_), channel_id=1, source_target_pairs={{0,1},{1,0},{2,3},{3,2},{4,5},{5,4},{6,7},{7,6},{8,9},{9,8},{10,11... | collective-permute-start | bytes 884744 | tf_op jit(solution)/shard_map/ppermute | solution.py:307
  30.9 13.3 %slice-start = ((s8[4718592]{0:T(1024)(128)(4,1)}), s8[4194304]{0:T(1024)(128)(4,1)S(1)}, s32[]{:S(2)}) async-start(s8[4718592]{0:T(1024)(128)(4,1)} %bitcast), calls=%async_computation | async-start | bytes 8388608
  33.3 10.8 %slice-start.1 = ((s8[4718592]{0:T(1024)(128)(4,1)}), s8[524288]{0:T(1024)(128)(4,1)S(1)}, s32[]{:S(2)}) async-start(s8[4718592]{0:T(1024)(128)(4,1)} %bitcast), calls=%async_computation.1 | async-start | bytes 1048576
  34.0 9.1 %collective-permute-start.13 = (bf16[64,384]{1,0:T(8,128)(2,1)S(1)}, bf16[64,384]{1,0:T(8,128)(2,1)S(1)}, u32[]{:S(2)}, u32[]{:S(2)}) collective-permute-start(bf16[64,384]{1,0:T(8,128)(2,1)S(1)} %get-tuple-element.49), channel_id=1, source_target_pairs={{0,12},{4,8},{8,4},{12,0},{1,13},{5,9},{9,5},{13,1},{2,14},{6,10},... | collective-permute-start | bytes 147464 | tf_op jit(solution)/shard_map/ppermute | solution.py:396
  38.0 6.2 %collective-permute-start.14 = (bf16[64,384]{1,0:T(8,128)(2,1)S(1)}, bf16[64,384]{1,0:T(8,128)(2,1)S(1)}, u32[]{:S(2)}, u32[]{:S(2)}) collective-permute-start(bf16[64,384]{1,0:T(8,128)(2,1)S(1)} %get-tuple-element.50), channel_id=1, source_target_pairs={{0,8},{4,12},{8,0},{12,4},{1,9},{5,13},{9,1},{13,5},{2,10},{6,14},... | collective-permute-start | bytes 147464 | tf_op jit(solution)/shard_map/ppermute | solution.py:396
  38.6 5.6 %collective-permute-start.15 = (bf16[64,384]{1,0:T(8,128)(2,1)S(1)}, bf16[64,384]{1,0:T(8,128)(2,1)S(1)}, u32[]{:S(2)}, u32[]{:S(2)}) collective-permute-start(bf16[64,384]{1,0:T(8,128)(2,1)S(1)} %get-tuple-element.51), channel_id=1, source_target_pairs={{0,4},{4,0},{8,12},{12,8},{1,5},{5,1},{9,13},{13,9},{2,6},{6,2},{1... | collective-permute-start | bytes 147464 | tf_op jit(solution)/shard_map/ppermute | solution.py:396
  39.7 7.8 %collective-permute-start.9 = (bf16[64,384]{1,0:T(8,128)(2,1)S(1)}, bf16[64,384]{1,0:T(8,128)(2,1)S(1)}, u32[]{:S(2)}, u32[]{:S(2)}) collective-permute-start(bf16[64,384]{1,0:T(8,128)(2,1)S(1)} %get-tuple-element.43), channel_id=1, source_target_pairs={{0,12},{4,8},{8,4},{12,0},{1,13},{5,9},{9,5},{13,1},{2,14},{6,10},... | collective-permute-start | bytes 147464 | tf_op jit(solution)/shard_map/ppermute | solution.py:396
  43.0 5.3 %collective-permute-start.10 = (bf16[64,384]{1,0:T(8,128)(2,1)S(1)}, bf16[64,384]{1,0:T(8,128)(2,1)S(1)}, u32[]{:S(2)}, u32[]{:S(2)}) collective-permute-start(bf16[64,384]{1,0:T(8,128)(2,1)S(1)} %get-tuple-element.44), channel_id=1, source_target_pairs={{0,8},{4,12},{8,0},{12,4},{1,9},{5,13},{9,1},{13,5},{2,10},{6,14},... | collective-permute-start | bytes 147464 | tf_op jit(solution)/shard_map/ppermute | solution.py:396
  43.1 5.3 %collective-permute-start.11 = (bf16[64,384]{1,0:T(8,128)(2,1)S(1)}, bf16[64,384]{1,0:T(8,128)(2,1)S(1)}, u32[]{:S(2)}, u32[]{:S(2)}) collective-permute-start(bf16[64,384]{1,0:T(8,128)(2,1)S(1)} %get-tuple-element.45), channel_id=1, source_target_pairs={{0,4},{4,0},{8,12},{12,8},{1,5},{5,1},{9,13},{13,9},{2,6},{6,2},{1... | collective-permute-start | bytes 147464 | tf_op jit(solution)/shard_map/ppermute | solution.py:396
  46.0 6.5 %collective-permute-start.16 = (bf16[32,3072]{1,0:T(8,128)(2,1)S(1)}, bf16[32,3072]{1,0:T(8,128)(2,1)S(1)}, u32[]{:S(2)}, u32[]{:S(2)}) collective-permute-start(bf16[32,3072]{1,0:T(8,128)(2,1)S(1)} %get-tuple-element.54), channel_id=1, source_target_pairs={{0,2},{2,0},{1,3},{3,1},{4,6},{6,4},{5,7},{7,5},{8,10},{10,8},{9,1... | collective-permute-start | bytes 589832 | tf_op jit(solution)/shard_map/ppermute | solution.py:307
  50.1 5.8 %collective-permute-start.12 = (bf16[32,3072]{1,0:T(8,128)(2,1)S(1)}, bf16[32,3072]{1,0:T(8,128)(2,1)S(1)}, u32[]{:S(2)}, u32[]{:S(2)}) collective-permute-start(bf16[32,3072]{1,0:T(8,128)(2,1)S(1)} %get-tuple-element.48), channel_id=1, source_target_pairs={{0,2},{2,0},{1,3},{3,1},{4,6},{6,4},{5,7},{7,5},{8,10},{10,8},{9,1... | collective-permute-start | bytes 589832 | tf_op jit(solution)/shard_map/ppermute | solution.py:307
